TPU v7x, 512 devices: a whole 4x4x16 slice. The times are simulated.
512 devices in a mesh: src: 16 (over y_hi, x, core), tgt: 32 (over z, y_lo).
Axes of the slice: x: 4, y: 4 (y_hi: 2, y_lo: 2; y = y_hi * 2 + y_lo), z: 16, core: 2. Of those that a mesh axis runs over, the one named last changes fastest.
Arguments:
- source: bfloat16 [16384, 64], P('src'), may hold values from -30 to 30
- target: bfloat16 [131072, 64], P('tgt'), may hold values from -6 to 6
- log_source: float32 [32, 16384], P(None, 'src'), may hold values from -6 to 6
- log_target: float32 [32, 131072], P(None, 'tgt'), may hold values from -6 to 6
Outputs:
- src_potential: float32 [32, 16384], P(None, 'src')
- tgt_potential: float32 [32, 131072], P(None, 'tgt')
All inputs are finite; a program needn't handle non-finite values.
Results may differ from a plain program's by a relative error of at most 0.00032.
Values sent between devices are 32-bit elements; how exact they have to be, the bound alone decides.
No kernel may reach another device: no remote copies, remote signals or barrier semaphores. Data moves between devices by JAX's collectives and lax.ppermute only.
A program may use at most 64 MiB of HBM per device.

v0:
```python
import jax
import jax.numpy as jnp
from jax import lax
from jax.sharding import PartitionSpec as P

FEAT = 64
ITERS = 2


entropy = 0.1


def cost_block(rows, cols):
    row_sq = jnp.sum(jnp.square(rows.astype(jnp.float32)), axis=1)
    col_sq = jnp.sum(jnp.square(cols.astype(jnp.float32)), axis=1)
    cross = jnp.dot(rows, cols.T, preferred_element_type=jnp.float32)
    return (row_sq[:, None] + col_sq[None, :] - 2.0 * cross) / FEAT


def lse_terms(cost, pot):
    top = jnp.max(pot, axis=0)
    shift = top[None, :] - cost / entropy
    peak = jnp.max(shift, axis=1)
    kernel = jnp.exp(shift - peak[:, None]).astype(jnp.bfloat16)
    weight = jnp.exp(pot - top[None, :]).astype(jnp.bfloat16)
    total = lax.dot_general(
        weight, kernel, (((1,), (1,)), ((), ())), preferred_element_type=jnp.float32
    )
    return (peak, total)


def local_terms(cells, others, pot):
    rows = cells.shape[0]
    block = min(256, rows)
    count = rows // block

    def one(index):
        part = lax.dynamic_slice_in_dim(cells, index * block, block, 0)
        return lse_terms(cost_block(part, others), pot)

    peaks, totals = lax.map(one, jnp.arange(count, dtype=jnp.int32))
    peaks = peaks.reshape(rows)
    totals = jnp.transpose(totals, (1, 0, 2)).reshape(totals.shape[1], rows)
    return (peaks, totals)


def body(source, target, log_source, log_target):
    tgt_potential = jnp.zeros(log_target.shape, jnp.float32)
    src_potential = jnp.zeros(log_source.shape, jnp.float32)
    for step in range(ITERS):
        peaks, totals = local_terms(source, target, tgt_potential / entropy + log_target)
        best = lax.pmax(peaks, "tgt")
        summed = lax.psum(totals * jnp.exp(peaks - best)[None, :], "tgt")
        src_potential = -entropy * (best[None, :] + jnp.log(summed))
        peaks, totals = local_terms(target, source, src_potential / entropy + log_source)
        best = lax.pmax(peaks, "src")
        summed = lax.psum(totals * jnp.exp(peaks - best)[None, :], "src")
        tgt_potential = -entropy * (best[None, :] + jnp.log(summed))
    return (src_potential, tgt_potential)


def solution(mesh):
    in_specs = (P("src", None), P("tgt", None), P(None, "src"), P(None, "tgt"))
    out_specs = (P(None, "src"), P(None, "tgt"))
    return jax.shard_map(body, mesh=mesh, in_specs=in_specs, out_specs=out_specs, check_vma=False)
```

profile of v0, /device:TPU:1, one launch (start us, length us, event | category | flops | bytes accessed | tf_op | source)
XLA Modules:
  0.0 1241.4 jit_solution(9055783020756354962)
XLA Ops:
  8.4 25.6 %while.56 = (s32[]{:T(128)}, f32[4,256]{1,0:T(4,128)S(1)}, f32[4,32,256]{2,1,0:T(8,128)S(1)}, f32[4096]{0:T(1024)S(1)}, s32[4]{0:T(128)S(1)}, /*index=5*/bf16[10...) while((s32[]{:T(128)}, f32[4,256]{1,0:T(4,128)S(1)}, ...), condition=%wide.region_5.6_spmd, body=%wide.region_1.5_spmd.sunk | while | flops 210808320 | bytes 12228827 | solution.py:41
  11.6 2.3 fusion.61
  18.0 2.3 fusion.61
  24.4 2.3 fusion.61
  30.8 2.3 fusion.61
  33.9 57.4 %pmax.28 = f32[1024]{0:T(1024)S(1)} all-reduce(f32[1024]{0:T(1024)S(1)} %bitcast.98), channel_id=1, replica_groups=mesh['src'=16,'tgt'=32] {'tgt'}, use_global_device_ids=true, to_apply=%region_6.7 | all-reduce | flops 1024 | bytes 8192 | tf_op jit(solution)/shard_map/pmax | solution.py:52
  92.1 243.1 %all-reduce.5.cloned.1.call-done = f32[32,1024]{1,0:T(8,128)} async-done(((f32[32,1024]{1,0:T(8,128)}), f32[32,1024]{1,0:T(8,128)}) %all-reduce.5.cloned.1.call-update) | async-done | bytes 131088 | tf_op jit(solution)/shard_map/psum | solution.py:53
  336.2 76.3 %while.57 = (s32[]{:T(128)}, f32[16,256]{1,0:T(8,128)S(1)}, f32[16,32,256]{2,1,0:T(8,128)S(1)}, f32[1024]{0:T(1024)S(1)}, s32[16]{0:T(128)S(1)}, /*index=5*/bf16...) while((s32[]{:T(128)}, f32[16,256]{1,0:T(8,128)S(1)}, ...), condition=%wide.region_13.14_spmd, body=%wide.region_9.0_spmd.sunk | while | flops 52738564 | bytes 2611391 | solution.py:41
  348.7 1.4 fusion.64
  353.5 1.4 fusion.64
  358.3 1.4 fusion.64
  363.0 1.4 fusion.64
  367.8 1.4 fusion.64
  372.6 1.4 fusion.64
  377.3 1.4 fusion.64
  382.1 1.4 fusion.64
  386.9 1.4 fusion.64
  391.6 1.4 fusion.64
  396.4 1.4 fusion.64
  401.2 1.4 fusion.64
  405.9 1.4 fusion.64
  410.7 1.4 fusion.64
  412.5 82.4 %pmax.29 = f32[4096]{0:T(1024)S(1)} all-reduce(f32[4096]{0:T(1024)S(1)} %bitcast.88), channel_id=1, replica_groups=mesh['src'=16,'tgt'=32] {'src'}, use_global_device_ids=true, to_apply=%region_14.15 | all-reduce | flops 4096 | bytes 32768 | tf_op jit(solution)/shard_map/pmax | solution.py:56
  495.9 152.8 %all-reduce.7.cloned.1.call-done = f32[32,4096]{1,0:T(8,128)} async-done(((f32[32,4096]{1,0:T(8,128)}), f32[32,4096]{1,0:T(8,128)}) %all-reduce.7.cloned.1.call-update) | async-done | bytes 524304 | tf_op jit(solution)/shard_map/psum | solution.py:57
  649.9 14.1 %while.58 = (s32[]{:T(128)}, f32[4,256]{1,0:T(4,128)S(1)}, f32[4,32,256]{2,1,0:T(8,128)S(1)}, f32[4096]{0:T(1024)S(1)}, s32[4]{0:T(128)S(1)}, /*index=5*/bf16[10...) while((s32[]{:T(128)}, f32[4,256]{1,0:T(4,128)S(1)}, ...), condition=%wide.region_21.22_spmd, body=%wide.region_17.21_spmd.sunk | while | flops 210808320 | bytes 10131647 | solution.py:41
  664.1 49.8 %pmax.30 = f32[1024]{0:T(1024)S(1)} all-reduce(f32[1024]{0:T(1024)S(1)} %bitcast.100), channel_id=1, replica_groups=mesh['src'=16,'tgt'=32] {'tgt'}, use_global_device_ids=true, to_apply=%region_22.23 | all-reduce | flops 1024 | bytes 8192 | tf_op jit(solution)/shard_map/pmax | solution.py:52
  714.6 243.5 %all-reduce.9.cloned.1.call-done = f32[32,1024]{1,0:T(8,128)} async-done(((f32[32,1024]{1,0:T(8,128)}), f32[32,1024]{1,0:T(8,128)}) %all-reduce.9.cloned.1.call-update) | async-done | bytes 131088 | tf_op jit(solution)/shard_map/psum | solution.py:53
  958.1 1.6 fusion.37
  959.8 37.1 %while.59 = (s32[]{:T(128)}, f32[16,256]{1,0:T(8,128)S(1)}, f32[16,32,256]{2,1,0:T(8,128)S(1)}, f32[1024]{0:T(1024)S(1)}, s32[16]{0:T(128)S(1)}, /*index=5*/bf16...) while((s32[]{:T(128)}, f32[16,256]{1,0:T(8,128)S(1)}, ...), condition=%wide.region_29.30_spmd, body=%wide.region_25.29_spmd.sunk | while | flops 52738564 | bytes 2611391 | solution.py:41
  996.9 82.3 %pmax.31 = f32[4096]{0:T(1024)S(1)} all-reduce(f32[4096]{0:T(1024)S(1)} %bitcast.90), channel_id=1, replica_groups=mesh['src'=16,'tgt'=32] {'src'}, use_global_device_ids=true, to_apply=%region_30.31 | all-reduce | flops 4096 | bytes 32768 | tf_op jit(solution)/shard_map/pmax | solution.py:56
  1080.1 152.8 %all-reduce.11.cloned.1.call-done = f32[32,4096]{1,0:T(8,128)} async-done(((f32[32,4096]{1,0:T(8,128)}), f32[32,4096]{1,0:T(8,128)}) %all-reduce.11.cloned.1.call-update) | async-done | bytes 524304 | tf_op jit(solution)/shard_map/psum | solution.py:57
  1232.9 1.9 add_multiply_fusion
  (277 shorter events, 103.4 us)
Async XLA Ops:
  7.2 328.0 %all-reduce.5.cloned.1.call-start = ((), (), s32[]{:S(2)}) async-start(), calls=%async_computation | async-start | bytes 262144 | tf_op jit(solution)/shard_map/psum | solution.py:53
  8.3 326.8 %copy-start.4 = (f32[32,1024]{1,0:T(8,128)S(1)}, f32[32,1024]{1,0:T(8,128)}, u32[]{:S(2)}) copy-start(f32[32,1024]{1,0:T(8,128)} %param.14) | copy-start | bytes 393220
  8.4 5.5 copy-start.1
  14.8 5.5 copy-start.1
  21.2 5.5 copy-start.1
  27.5 5.5 copy-start.1
  92.1 556.6 %all-reduce.7.cloned.1.call-start = ((), (), s32[]{:S(2)}) async-start(), calls=%async_computation.1 | async-start | bytes 1048576 | tf_op jit(solution)/shard_map/psum | solution.py:57
  336.2 312.5 %copy-start.2 = (f32[32,4096]{1,0:T(8,128)S(1)}, f32[32,4096]{1,0:T(8,128)}, u32[]{:S(2)}) copy-start(f32[32,4096]{1,0:T(8,128)} %get-tuple-element.836) | copy-start | bytes 1572868
  412.5 237.4 %copy-start = (bf16[4096,64]{0,1:T(8,128)(2,1)S(1)}, bf16[4096,64]{0,1:T(8,128)(2,1)}, u32[]{:S(2)}) copy-start(bf16[4096,64]{0,1:T(8,128)(2,1)} %get-tuple-element.834) | copy-start | bytes 1572868
  412.5 237.4 %copy-start.3 = (bf16[1024,64]{0,1:T(8,128)(2,1)S(1)}, bf16[1024,64]{0,1:T(8,128)(2,1)}, u32[]{:S(2)}) copy-start(bf16[1024,64]{0,1:T(8,128)(2,1)} %get-tuple-element.838) | copy-start | bytes 393220
  495.9 462.2 %all-reduce.9.cloned.1.call-start = ((), (), s32[]{:S(2)}) async-start(), calls=%async_computation.2 | async-start | bytes 262144 | tf_op jit(solution)/shard_map/psum | solution.py:53
  714.6 518.3 %all-reduce.11.cloned.1.call-start = ((), (), s32[]{:S(2)}) async-start(), calls=%async_computation.3 | async-start | bytes 1048576 | tf_op jit(solution)/shard_map/psum | solution.py:57
Sparse Core Ops, SparseCore 0:
  92.2 242.9 all-reduce.4
  496.0 152.6 all-reduce.6
  714.7 243.3 all-reduce.8
  1080.2 152.6 all-reduce.10
where the time goes:
time: 1240 us
  waiting for transfers between devices  792 us (64%)
  blocking collectives  272 us (22%)
  matrix products  61.7 us (5%)
  other arithmetic  47.1 us (4%)
  loops' own time  27.9 us (2%)
  local copies, waits for them, and re-layouts  26.3 us (2%)
  between operations  14 us (1%)
    psum x2, waiting for transfers between devices, body(): summed = lax.psum(totals * jnp.exp(peaks - best)[None, :], 'tgt')  487 us
    psum x2, waiting for transfers between devices, body(): summed = lax.psum(totals * jnp.exp(peaks - best)[None, :], 'src')  306 us
    pmax x2, blocking collectives, body(): best = lax.pmax(peaks, 'src')  165 us
    pmax x2, blocking collectives, body(): best = lax.pmax(peaks, 'tgt')  107 us
    dot_general x40, matrix products, cost_block(): cross = jnp.dot(rows, cols.T, preferred_element_type=jnp.float32)  43.8 us
    another operation x4, loops' own time, local_terms(): peaks, totals = lax.map(one, jnp.arange(count, dtype=jnp.int32))  27.9 us
  transfers between devices with their start and end apart: 4, of which 4 were waited for; matrix products, arithmetic and copies ran while one was open for 0% of the time, Pallas kernels for 0%

commit v1 on v0

v1 whole, which is shorter than its diff:
```python
import functools
import math

import jax
import jax.numpy as jnp
from jax import lax
from jax.experimental import pallas as pl
from jax.experimental.pallas import tpu as pltpu
from jax.sharding import Mesh
from jax.sharding import PartitionSpec as P

FEAT = 64
ITERS = 2
PAIRS = 32
LANES = 128

entropy = 0.1

LOG2E = math.log2(math.e)
HALF = LOG2E / (FEAT * entropy)
SCALE = 2.0 * HALF
BACK = -entropy / LOG2E

NEAR = ("zl", "yl")
FAR = ("zh",)
SRC = ("yh", "x", "core")

COLS = 256
CHUNK = 512


def pieces(value):
    high = value.astype(jnp.bfloat16)
    rest = value - high.astype(jnp.float32)
    middle = rest.astype(jnp.bfloat16)
    low = (rest - middle.astype(jnp.float32)).astype(jnp.bfloat16)
    return (high, middle, low)


def square_norms(cells):
    square = jnp.square(cells.astype(jnp.float32))
    high = square.astype(jnp.bfloat16)
    low = (square - high.astype(jnp.float32)).astype(jnp.bfloat16)
    both = jnp.concatenate([high, low], axis=1)
    ones = jnp.ones((8, both.shape[1]), jnp.bfloat16)
    sums = lax.dot_general(ones, both, (((1,), (1,)), ((), ())), preferred_element_type=jnp.float32)
    return sums[:1]


def update_kernel(first, emit, *refs):
    refs = list(refs)
    others_ref, cells_ref, log_ref = refs[:3]
    refs = refs[3:]
    known_ref = None if first else refs.pop(0)
    out_ref = refs.pop(0)
    pot_ref = refs.pop(0) if emit else None
    norm_ref = refs.pop(0) if first else None
    left_ref, right_ref, weight_ref = refs

    others = others_ref.shape[0]
    cells = cells_ref.shape[0]
    rows = others // LANES

    scaled = cells_ref[...].astype(jnp.float32) * SCALE
    high, middle, low = pieces(scaled)
    lane = lax.broadcasted_iota(jnp.int32, (cells, FEAT), 1)
    ones = jnp.where(lane < 3, 1.0, 0.0).astype(jnp.bfloat16)
    right_ref[:, :LANES] = jnp.concatenate([high, middle], axis=1)
    right_ref[:, LANES:] = jnp.concatenate([ones, low], axis=1)

    if first or emit:
        norms = square_norms(others_ref[...]) * HALF
    if first:
        norm_ref[...] = jnp.broadcast_to(norms, norm_ref.shape)

    for row in range(rows):
        part = slice(row * LANES, (row + 1) * LANES)
        pot = log_ref[:, part] * LOG2E
        if not first:
            known = known_ref[pl.ds(row, PAIRS, stride=rows), :]
            pot = pot - known
        if emit:
            pot_ref[:, part] = (known - norms[:, part]) * BACK
        top = jnp.max(pot, axis=0, keepdims=True)
        weight_ref[:, part] = jnp.exp2(pot - top).astype(jnp.bfloat16)
        bias = top - norms[:, part] if first else top
        high, middle, low = pieces(bias)
        at = lax.broadcasted_iota(jnp.int32, (8, LANES), 0)
        high, middle, low = (jnp.broadcast_to(x.astype(jnp.float32), (8, LANES)) for x in (high, middle, low))
        block = jnp.where(at == 0, high, jnp.where(at == 1, middle, jnp.where(at == 2, low, 0.0)))
        block = jnp.concatenate([block, jnp.zeros((LANES - 8, LANES), jnp.float32)], axis=0)
        turned = block.T.astype(jnp.bfloat16)
        feats = others_ref[part, :]
        left_ref[part, :LANES] = jnp.concatenate([feats, feats], axis=1)
        left_ref[part, LANES:] = jnp.concatenate([turned[:, :FEAT], feats], axis=1)

    def tile(index, carry):
        start = pl.multiple_of(index * COLS, COLS)
        right = right_ref[pl.ds(start, COLS), :]
        peak = total = None
        for at in range(0, others, CHUNK):
            part = slice(at, at + CHUNK)
            shift = lax.dot_general(
                left_ref[part, :], right, (((1,), (1,)), ((), ())), preferred_element_type=jnp.float32
            )
            best = jnp.max(shift, axis=0, keepdims=True)
            if peak is not None:
                best = jnp.maximum(best, peak)
            kernel = jnp.exp2(shift - best).astype(jnp.bfloat16)
            sums = jnp.dot(weight_ref[:, part], kernel, preferred_element_type=jnp.float32)
            total = sums if peak is None else total * jnp.exp2(peak - best) + sums
            peak = best
        result = peak + jnp.log2(total)
        stride = cells // LANES
        for k in range(COLS // LANES):
            out_ref[pl.ds(index * (COLS // LANES) + k, PAIRS, stride=stride), :] = result[:, k * LANES : (k + 1) * LANES]
        return carry

    lax.fori_loop(0, cells // COLS, tile, 0)


def update(others, cells, log, known=None, emit=False):
    first = known is None
    count, own = others.shape[0], cells.shape[0]
    out = [jax.ShapeDtypeStruct((PAIRS * own // LANES, LANES), jnp.float32)]
    if emit:
        out.append(jax.ShapeDtypeStruct((PAIRS, count), jnp.float32))
    if first:
        out.append(jax.ShapeDtypeStruct((8, count), jnp.float32))
    args = [others, cells, log] + ([] if first else [known])
    return pl.pallas_call(
        functools.partial(update_kernel, first, emit),
        out_shape=out,
        scratch_shapes=[
            pltpu.VMEM((count, 2 * LANES), jnp.bfloat16),
            pltpu.VMEM((own, 2 * LANES), jnp.bfloat16),
            pltpu.VMEM((PAIRS, count), jnp.bfloat16),
        ],
        compiler_params=pltpu.CompilerParams(vmem_limit_bytes=40 * 1024 * 1024),
    )(*args)


def log_sum(parts):
    best = jnp.max(parts, axis=0)
    return best + jnp.log2(jnp.sum(jnp.exp2(parts - best[None]), axis=0))


def exchange(value, axes):
    return lax.all_to_all(value, axes, 0, 0)


def spread(value, axes, count):
    return exchange(jnp.broadcast_to(value[None], (count,) + value.shape), axes)


def over_targets(parts, sizes):
    near = sizes["zl"] * sizes["yl"]
    rows = parts.shape[0]
    mine = log_sum(exchange(parts.reshape(near, rows // near, LANES), NEAR))
    mine = log_sum(spread(mine, FAR, sizes["zh"]))
    return spread(mine, NEAR, near).reshape(rows, LANES)


def over_sources(parts, sizes):
    group = sizes["yh"] * sizes["x"] * sizes["core"]
    rows = parts.shape[0]
    mine = log_sum(exchange(parts.reshape(group, rows // group, LANES), SRC))
    return spread(mine, SRC, group).reshape(rows, LANES)


def body(sizes, source, target, log_source, log_target):
    parts, norms = update(target, source, log_target)
    for step in range(ITERS):
        if step:
            (parts,) = update(target, source, log_target, known)
        known = over_targets(parts, sizes)
        if step < ITERS - 1:
            (parts,) = update(source, target, log_source, known)
        else:
            parts, src_potential = update(source, target, log_source, known, emit=True)
        known = over_sources(parts, sizes)
    tgt_potential = (known.reshape(PAIRS, -1) - norms[:1]) * BACK
    return (src_potential, tgt_potential)


def solution(mesh):
    sizes = {"yh": 2, "x": 4, "core": 2, "zh": 4, "zl": 4, "yl": 2}
    fine = Mesh(mesh.devices.reshape(tuple(sizes.values())), tuple(sizes))
    src, tgt = SRC, FAR + NEAR
    in_specs = (P(src, None), P(tgt, None), P(None, src), P(None, tgt))
    out_specs = (P(None, src), P(None, tgt))
    return jax.shard_map(
        functools.partial(body, sizes), mesh=fine, in_specs=in_specs, out_specs=out_specs, check_vma=False
    )
```

time: 1240 us -> 215 us (0.17)
  waiting for transfers between devices: 792 us -> 11.5 us
  blocking collectives: 272 us -> 133 us
  matrix products: 61.7 us -> 0 us
  Pallas kernels: 0 us -> 59.3 us
  other arithmetic: 47.1 us -> 1.34 us
  loops' own time: 27.9 us -> 0 us
  local copies, waits for them, and re-layouts: 26.3 us -> 3.69 us
  between operations: 14 us -> 0.84 us
    psum x4 -> x0, waiting for transfers between devices: 792 us -> none  [the longest x2 487 us: body(): summed = lax.psum(totals * jnp.exp(peaks - best)[None, :], 'tgt')]
    pmax x4 -> x0, blocking collectives: 272 us -> none  [the longest x2 165 us: body(): best = lax.pmax(peaks, 'src')]
    all_to_all x0 -> x9, blocking collectives: none -> 133 us  [exchange(): return lax.all_to_all(value, axes, 0, 0)]
    dot_general x80 -> x0, matrix products: 61.7 us -> none  [the longest x40 43.8 us: cost_block(): cross = jnp.dot(rows, cols.T, preferred_element_type=jnp.float32)]
    pallas_call x0 -> x4, Pallas kernels: none -> 59.3 us  [update(): pl.pallas_call(functools.partial(update_kernel, first, emit), out_shape=o...]
    reduce_sum x80 -> x6, other arithmetic: 37.3 us -> 0.31 us  [log_sum(): return best + jnp.log2(jnp.sum(jnp.exp2(parts - best[None]), axis=0))]
    another operation x4 -> x0, loops' own time: 27.9 us -> none  [local_terms(): peaks, totals = lax.map(one, jnp.arange(count, dtype=jnp.int32))]
    dynamic_slice x40 -> x0, local copies, waits for them, and re-layouts: 24.7 us -> none  [local_terms(): peaks, totals = lax.map(one, jnp.arange(count, dtype=jnp.int32))]
  transfers between devices with their start and end apart: 4 -> 1, of which waited for: 4 -> 1; matrix products, arithmetic and copies ran while one was open for 0% -> 0% of each run, Pallas kernels for 0% -> 0%
where the time goes in v1:
time: 215 us
  blocking collectives  133 us (62%)
  Pallas kernels  59.3 us (28%)
  waiting for transfers between devices  11.5 us (5%)
  starting transfers between devices  4.44 us (2%)
  local copies, waits for them, and re-layouts  3.69 us (2%)
    all_to_all x9, blocking collectives, exchange(): return lax.all_to_all(value, axes, 0, 0)  133 us
    pallas_call x4, Pallas kernels, update(): pl.pallas_call(functools.partial(update_kernel, first, emit), out_shape=o...  59.3 us
    all_to_all x1, waiting for transfers between devices, exchange(): return lax.all_to_all(value, axes, 0, 0)  11.5 us
    all_to_all x1, starting transfers between devices, exchange(): return lax.all_to_all(value, axes, 0, 0)  4.44 us
  transfers between devices with their start and end apart: 1, of which 1 were waited for; matrix products, arithmetic and copies ran while one was open for 0% of the time, Pallas kernels for 0%

profile of v1, /device:TPU:1, one launch (start us, length us, event | category | flops | bytes accessed | tf_op | source)
XLA Modules:
  0.0 214.5 jit_solution(5557439902593749433)
XLA Ops:
  0.6 1.1 copy.20.refs_1_.refs_0_
  1.7 0.0 copy-start
  1.7 1.6 copy.21.refs_0_.refs_1_
  3.3 0.0 copy-done
  3.3 12.6 %shard_map.59 = (f32[256,128]{1,0:T(8,128)S(1)}, f32[8,4096]{1,0:T(8,128)S(1)}) custom-call(bf16[4096,64]{1,0:T(8,128)(2,1)S(1)} %copy.21.refs_0_.refs_1_, bf16[1024,64]{1,0:T(8,128)(2,1)S(1)} %copy.20.refs_1_.refs_0_, f32[32,4096]{1,0:T(8,128)S(1)} %copy-done), custom_call_target="tpu_custom_call" | custom-call | tf_op jit(solution)/shard_map/pallas_call | solution.py:131
  15.9 13.6 %all_to_all.50 = f32[8,32,128]{2,1,0:T(8,128)S(1)} all-to-all(f32[8,32,128]{2,1,0:T(8,128)S(1)} %bitcast.14), channel_id=1, replica_groups=mesh['yh'=2,'x'=4,'core'=2,'zh'=4,'zl'=4,'yl'=2] {'zl','yl'}, dimensions={0} | all-to-all | bytes 262144 | tf_op jit(solution)/shard_map/all_to_all | solution.py:149
  29.6 23.9 %all_to_all.51 = f32[4,32,128]{2,1,0:T(8,128)S(1)} all-to-all(f32[4,32,128]{2,1,0:T(8,128)S(1)} %broadcast_in_dim.12), channel_id=1, replica_groups=mesh['yh'=2,'x'=4,'core'=2,'zh'=4,'zl'=4,'yl'=2] {'zh'}, dimensions={0} | all-to-all | bytes 131072 | tf_op jit(solution)/shard_map/all_to_all | solution.py:149
  53.6 0.0 copy-start.1
  53.6 8.7 %all_to_all.52 = f32[8,32,128]{2,1,0:T(8,128)S(1)} all-to-all(f32[8,32,128]{2,1,0:T(8,128)S(1)} %broadcast_in_dim.13), channel_id=1, replica_groups=mesh['yh'=2,'x'=4,'core'=2,'zh'=4,'zl'=4,'yl'=2] {'zl','yl'}, dimensions={0} | all-to-all | bytes 262144 | tf_op jit(solution)/shard_map/all_to_all | solution.py:149
  62.3 0.0 copy-done.1
  62.3 17.2 %shard_map.60 = f32[1024,128]{1,0:T(8,128)S(1)} custom-call(bf16[1024,64]{1,0:T(8,128)(2,1)S(1)} %copy.20.refs_1_.refs_0_, bf16[4096,64]{1,0:T(8,128)(2,1)S(1)} %copy.21.refs_0_.refs_1_, f32[32,1024]{1,0:T(8,128)S(1)} %copy-done.1, f32[256,128]{1,0:T(8,128)S(1)} %bitcast.11), custom_call_target="tpu_custom_call" | custom-call | tf_op jit(solution)/shard_map/pallas_call | solution.py:131
  79.5 22.2 %all_to_all.53 = f32[16,64,128]{2,1,0:T(8,128)S(1)} all-to-all(f32[16,64,128]{2,1,0:T(8,128)S(1)} %bitcast.9), channel_id=1, replica_groups=mesh['yh'=2,'x'=4,'core'=2,'zh'=4,'zl'=4,'yl'=2] {'yh','x','core'}, dimensions={0} | all-to-all | bytes 1048576 | tf_op jit(solution)/shard_map/all_to_all | solution.py:149
  101.8 0.1 exponential_reduce_fusion.1
  102.0 15.0 %all_to_all.54 = f32[16,64,128]{2,1,0:T(8,128)S(1)} all-to-all(f32[16,64,128]{2,1,0:T(8,128)S(1)} %broadcast_in_dim.14), channel_id=1, replica_groups=mesh['yh'=2,'x'=4,'core'=2,'zh'=4,'zl'=4,'yl'=2] {'yh','x','core'}, dimensions={0} | all-to-all | bytes 1048576 | tf_op jit(solution)/shard_map/all_to_all | solution.py:149
  117.0 12.2 %shard_map.61 = f32[256,128]{1,0:T(8,128)S(1)} custom-call(bf16[4096,64]{1,0:T(8,128)(2,1)S(1)} %copy.21.refs_0_.refs_1_, bf16[1024,64]{1,0:T(8,128)(2,1)S(1)} %copy.20.refs_1_.refs_0_, f32[32,4096]{1,0:T(8,128)S(1)} %copy-done, f32[1024,128]{1,0:T(8,128)S(1)} %bitcast.8), custom_call_target="tpu_custom_call" | custom-call | tf_op jit(solution)/shard_map/pallas_call | solution.py:131
  129.1 8.7 %all_to_all.55 = f32[8,32,128]{2,1,0:T(8,128)S(1)} all-to-all(f32[8,32,128]{2,1,0:T(8,128)S(1)} %bitcast.12), channel_id=1, replica_groups=mesh['yh'=2,'x'=4,'core'=2,'zh'=4,'zl'=4,'yl'=2] {'zl','yl'}, dimensions={0} | all-to-all | bytes 262144 | tf_op jit(solution)/shard_map/all_to_all | solution.py:149
  137.9 14.3 %all_to_all.56 = f32[4,32,128]{2,1,0:T(8,128)S(1)} all-to-all(f32[4,32,128]{2,1,0:T(8,128)S(1)} %broadcast_in_dim.15), channel_id=1, replica_groups=mesh['yh'=2,'x'=4,'core'=2,'zh'=4,'zl'=4,'yl'=2] {'zh'}, dimensions={0} | all-to-all | bytes 131072 | tf_op jit(solution)/shard_map/all_to_all | solution.py:149
  152.2 8.6 %all_to_all.57 = f32[8,32,128]{2,1,0:T(8,128)S(1)} all-to-all(f32[8,32,128]{2,1,0:T(8,128)S(1)} %broadcast_in_dim.16), channel_id=1, replica_groups=mesh['yh'=2,'x'=4,'core'=2,'zh'=4,'zl'=4,'yl'=2] {'zl','yl'}, dimensions={0} | all-to-all | bytes 262144 | tf_op jit(solution)/shard_map/all_to_all | solution.py:149
  160.8 17.4 %shard_map.62 = (f32[1024,128]{1,0:T(8,128)S(1)}, f32[32,1024]{1,0:T(8,128)}) custom-call(bf16[1024,64]{1,0:T(8,128)(2,1)S(1)} %copy.20.refs_1_.refs_0_, bf16[4096,64]{1,0:T(8,128)(2,1)S(1)} %copy.21.refs_0_.refs_1_, f32[32,1024]{1,0:T(8,128)S(1)} %copy-done.1, f32[256,128]{1,0:T(8,128)S(1)} %bitcast.10), custom_call_target="tpu_custom_call" | custom-call | tf_op jit(solution)/shard_map/pallas_call | solution.py:131
  178.2 18.5 %all_to_all.58 = f32[16,64,128]{2,1,0:T(8,128)S(1)} all-to-all(f32[16,64,128]{2,1,0:T(8,128)S(1)} %bitcast.13), channel_id=1, replica_groups=mesh['yh'=2,'x'=4,'core'=2,'zh'=4,'zl'=4,'yl'=2] {'yh','x','core'}, dimensions={0} | all-to-all | bytes 1048576 | tf_op jit(solution)/shard_map/all_to_all | solution.py:149
  196.7 0.1 exponential_reduce_fusion
  196.8 0.8 broadcast_in_dim.17
  197.7 4.4 %all-to-all-start.9 = ((f32[16,64,128]{2,1,0:T(8,128)}), f32[16,64,128]{2,1,0:T(8,128)S(1)}, u32[]{:S(2)}, u32[]{:S(2)}) async-start(f32[16,64,128]{2,1,0:T(8,128)} %broadcast_in_dim.17), calls=%async_computation.9 | async-start | bytes 1048576 | tf_op jit(solution)/shard_map/all_to_all | solution.py:149
  202.1 11.5 %all-to-all-done.9 = f32[16,64,128]{2,1,0:T(8,128)S(1)} async-done(((f32[16,64,128]{2,1,0:T(8,128)}), f32[16,64,128]{2,1,0:T(8,128)S(1)}, u32[]{:S(2)}, u32[]{:S(2)}) %all-to-all-start.9) | async-done | bytes 524320 | tf_op jit(solution)/shard_map/all_to_all | solution.py:149
  213.6 0.1 reshape_reshape.3
  213.7 0.8 subtract_multiply_fusion
  (22 shorter events, 0.4 us)
Async XLA Ops:
  1.7 1.6 copy-start
  53.6 8.7 %copy-start.1 = (f32[32,1024]{1,0:T(8,128)S(1)}, f32[32,1024]{1,0:T(8,128)}, u32[]{:S(2)}) copy-start(f32[32,1024]{1,0:T(8,128)} %refs_2_.7) | copy-start | bytes 393220
  197.7 15.9 %all-to-all-start.9 = ((f32[16,64,128]{2,1,0:T(8,128)}), f32[16,64,128]{2,1,0:T(8,128)S(1)}, u32[]{:S(2)}, u32[]{:S(2)}) async-start(f32[16,64,128]{2,1,0:T(8,128)} %broadcast_in_dim.17), calls=%async_computation.9 | async-start | bytes 1048576 | tf_op jit(solution)/shard_map/all_to_all | solution.py:149

commit v2 on v1

v2 whole, which is shorter than its diff:
```python
import functools
import math

import jax
import jax.numpy as jnp
from jax import lax
from jax.experimental import pallas as pl
from jax.experimental.pallas import tpu as pltpu
from jax.sharding import Mesh
from jax.sharding import PartitionSpec as P

FEAT = 64
ITERS = 2
PAIRS = 32
LANES = 128
DEPTH = 256

entropy = 0.1

LOG2E = math.log2(math.e)
HALF = LOG2E / (FEAT * entropy)
SCALE = 2.0 * HALF
BACK = -entropy / LOG2E
SMALL = 2.0**-90

NEAR = ("zl", "yl")
FAR = ("zh",)
SRC = ("yh", "x", "core")

TILE = 256
CHUNK = 512


def pieces(value):
    high = value.astype(jnp.bfloat16)
    rest = value - high.astype(jnp.float32)
    middle = rest.astype(jnp.bfloat16)
    low = (rest - middle.astype(jnp.float32)).astype(jnp.bfloat16)
    return (high, middle, low)


def half_norms(feats):
    return jnp.sum(jnp.square(feats.astype(jnp.float32)), axis=0, keepdims=True) * HALF


def fill_left(left_ref, cells_ref):
    for at in range(0, left_ref.shape[0], LANES):
        part = slice(at, at + LANES)
        scaled = cells_ref[:, part].astype(jnp.float32) * SCALE
        row = lax.broadcasted_iota(jnp.int32, (LANES - FEAT, LANES), 0)
        ones = jnp.where(row < 3, 1.0, 0.0)
        high, middle, low = (x.astype(jnp.float32) for x in pieces(scaled))
        left_ref[part, :LANES] = jnp.concatenate([high, middle], axis=0).T.astype(jnp.bfloat16)
        left_ref[part, LANES:] = jnp.concatenate([low, ones], axis=0).T.astype(jnp.bfloat16)


def fill_right(right_ref, others_ref, bias):
    count = others_ref.shape[1]
    feats = others_ref[...]
    for k in range(3):
        right_ref[k * FEAT : (k + 1) * FEAT, :] = feats
    row = lax.broadcasted_iota(jnp.int32, (16, count), 0)
    high, middle, low = (jnp.broadcast_to(x.astype(jnp.float32), (16, count)) for x in pieces(bias))
    block = jnp.where(row == 0, high, jnp.where(row == 1, middle, jnp.where(row == 2, low, 0.0)))
    right_ref[3 * FEAT : 3 * FEAT + 16, :] = block.astype(jnp.bfloat16)
    right_ref[3 * FEAT + 16 :, :] = jnp.zeros((DEPTH - 3 * FEAT - 16, count), jnp.bfloat16)


def as_row(column):
    rows = column.shape[0]
    return jnp.broadcast_to(column, (rows, LANES)).T[:1]


def first_kernel(target_ref, source_ref, log_ref, out_ref, kept_ref, peak_ref, bias_ref, norm_ref,
                 left_ref, right_ref, weight_ref, shift_ref):
    cells, others = kept_ref.shape
    fill_left(left_ref, source_ref)
    norms = half_norms(target_ref[...])
    norm_ref[...] = jnp.broadcast_to(norms, norm_ref.shape)
    pot = log_ref[...] * LOG2E
    top = jnp.max(pot, axis=0, keepdims=True)
    weight_ref[...] = jnp.exp2(pot - top).astype(jnp.bfloat16)
    bias = top - norms
    bias_ref[...] = jnp.broadcast_to(bias, bias_ref.shape)
    fill_right(right_ref, target_ref, bias)

    def scores(tile):
        best = None
        for at in range(0, others, CHUNK):
            part = slice(at, at + CHUNK)
            shift = jnp.dot(left_ref[tile * TILE : (tile + 1) * TILE, :], right_ref[:, part],
                            preferred_element_type=jnp.float32)
            shift_ref[tile % 2, :, part] = shift
            for k in range(0, CHUNK, LANES):
                best = shift[:, k : k + LANES] if best is None else jnp.maximum(best, shift[:, k : k + LANES])
        return jnp.max(best, axis=1, keepdims=True)

    tiles = cells // TILE
    peak = scores(0)
    for tile in range(tiles):
        rows = slice(tile * TILE, (tile + 1) * TILE)
        after = scores(tile + 1) if tile + 1 < tiles else None
        total = None
        for at in range(0, others, CHUNK):
            part = slice(at, at + CHUNK)
            kernel = jnp.exp2(shift_ref[tile % 2, :, part] - peak).astype(jnp.bfloat16)
            kept_ref[rows, part] = kernel
            sums = lax.dot_general(weight_ref[:, part], kernel, (((1,), (1,)), ((), ())),
                                   preferred_element_type=jnp.float32)
            total = sums if total is None else total + sums
        for k in range(TILE // LANES):
            part = slice(tile * TILE + k * LANES, tile * TILE + (k + 1) * LANES)
            row = as_row(peak[k * LANES : (k + 1) * LANES])
            peak_ref[:, part] = jnp.broadcast_to(row, (8, LANES))
            result = row + jnp.log2(total[:, k * LANES : (k + 1) * LANES])
            out_ref[pl.ds(tile * (TILE // LANES) + k, PAIRS, stride=cells // LANES), :] = result
        peak = after


def again(out_ref, cells_ref, others_ref, pot_ref, left_ref, right_ref, weight_ref):
    cells, others = left_ref.shape[0], right_ref.shape[1]
    fill_left(left_ref, cells_ref)
    pot = pot_ref[...]
    top = jnp.max(pot, axis=0, keepdims=True)
    weight_ref[...] = jnp.exp2(pot - top).astype(jnp.bfloat16)
    fill_right(right_ref, others_ref, top)

    def tile(index, carry):
        rows = left_ref[pl.ds(pl.multiple_of(index * LANES, LANES), LANES), :]

        def chunk(step, carry):
            peak, total = carry
            part = pl.ds(pl.multiple_of(step * CHUNK, CHUNK), CHUNK)
            shift = jnp.dot(rows, right_ref[:, part], preferred_element_type=jnp.float32)
            best = jnp.maximum(peak, jnp.broadcast_to(jnp.max(shift, axis=1, keepdims=True), peak.shape))
            kernel = jnp.exp2(shift - best[:, :1]).astype(jnp.bfloat16)
            sums = lax.dot_general(weight_ref[:, part], kernel, (((1,), (1,)), ((), ())),
                                   preferred_element_type=jnp.float32)
            return best, total * jnp.exp2(peak - best).T[:1] + sums

        start = (jnp.full((LANES, LANES), -jnp.inf, jnp.float32), jnp.zeros((PAIRS, LANES), jnp.float32))
        peak, total = lax.fori_loop(0, others // CHUNK, chunk, start)
        out_ref[pl.ds(index, PAIRS, stride=cells // LANES), :] = peak.T[:1] + jnp.log2(total)
        return carry

    lax.fori_loop(0, cells // LANES, tile, 0)


def log_sums_of(known_ref, log_ref, pot_ref):
    rows = log_ref.shape[1] // LANES
    for row in range(rows):
        part = slice(row * LANES, (row + 1) * LANES)
        pot_ref[:, part] = log_ref[:, part] * LOG2E - known_ref[pl.ds(row, PAIRS, stride=rows), :]


def next_kernel(to_source, emit, *refs):
    refs = list(refs)
    cells_ref, others_ref, log_ref, known_ref, kept_ref, peak_ref, bias_ref, out_ref = refs[:8]
    refs = refs[8:]
    pot_out = refs.pop(0) if emit else None
    pot_ref, left_ref, right_ref, weight_ref = refs
    cells, others = left_ref.shape[0], right_ref.shape[1]

    log_sums_of(known_ref, log_ref, pot_ref)
    if emit:
        norms = half_norms(others_ref[...])
        rows = others // LANES
        for row in range(rows):
            part = slice(row * LANES, (row + 1) * LANES)
            pot_out[:, part] = (known_ref[pl.ds(row, PAIRS, stride=rows), :] - norms[:, part]) * BACK
    pot = pot_ref[...]
    scaled = pot - bias_ref[:1] if to_source else pot + peak_ref[:1]
    most = jnp.max(jnp.max(scaled, axis=0, keepdims=True), axis=1, keepdims=True)
    weight_ref[...] = jnp.exp2(scaled - most).astype(jnp.bfloat16)
    least = None
    for at in range(0, cells, TILE):
        if to_source:
            total = lax.dot_general(weight_ref[...], kept_ref[at : at + TILE, :], (((1,), (1,)), ((), ())),
                                    preferred_element_type=jnp.float32)
        else:
            total = jnp.dot(weight_ref[...], kept_ref[:, at : at + TILE], preferred_element_type=jnp.float32)
        least = total if least is None else jnp.minimum(least, total)
        for k in range(TILE // LANES):
            part = slice(at + k * LANES, at + (k + 1) * LANES)
            back = peak_ref[:1, part] if to_source else -bias_ref[:1, part]
            result = (back + most) + jnp.log2(total[:, k * LANES : (k + 1) * LANES])
            out_ref[pl.ds(part.start // LANES, PAIRS, stride=cells // LANES), :] = result
    least = jnp.min(least)

    @pl.when(jnp.logical_not(least >= SMALL))
    def _():
        again(out_ref, cells_ref, others_ref, pot_ref, left_ref, right_ref, weight_ref)


LIMIT = pltpu.CompilerParams(vmem_limit_bytes=28 * 1024 * 1024)


def first_update(target, source, log):
    others, cells = target.shape[1], source.shape[1]
    return pl.pallas_call(
        first_kernel,
        out_shape=[
            jax.ShapeDtypeStruct((PAIRS * cells // LANES, LANES), jnp.float32),
            jax.ShapeDtypeStruct((cells, others), jnp.bfloat16),
            jax.ShapeDtypeStruct((8, cells), jnp.float32),
            jax.ShapeDtypeStruct((8, others), jnp.float32),
            jax.ShapeDtypeStruct((8, others), jnp.float32),
        ],
        scratch_shapes=[
            pltpu.VMEM((cells, DEPTH), jnp.bfloat16),
            pltpu.VMEM((DEPTH, others), jnp.bfloat16),
            pltpu.VMEM((PAIRS, others), jnp.bfloat16),
            pltpu.VMEM((2, TILE, others), jnp.float32),
        ],
        compiler_params=LIMIT,
    )(target, source, log)


def next_update(cells, others, log, known, kept, to_source, emit=False):
    own, count = cells.shape[1], others.shape[1]
    out = [jax.ShapeDtypeStruct((PAIRS * own // LANES, LANES), jnp.float32)]
    if emit:
        out.append(jax.ShapeDtypeStruct((PAIRS, count), jnp.float32))
    return pl.pallas_call(
        functools.partial(next_kernel, to_source, emit),
        out_shape=out,
        scratch_shapes=[
            pltpu.VMEM((PAIRS, count), jnp.float32),
            pltpu.VMEM((own, DEPTH), jnp.bfloat16),
            pltpu.VMEM((DEPTH, count), jnp.bfloat16),
            pltpu.VMEM((PAIRS, count), jnp.bfloat16),
        ],
        compiler_params=LIMIT,
    )(cells, others, log, known, *kept)


def log_sum(parts):
    best = jnp.max(parts, axis=0)
    return best + jnp.log2(jnp.sum(jnp.exp2(parts - best[None]), axis=0))


def exchange(value, axes):
    return lax.all_to_all(value, axes, 0, 0)


def spread(value, axes, count):
    return exchange(jnp.broadcast_to(value[None], (count,) + value.shape), axes)


def over_targets(parts, sizes):
    near = sizes["zl"] * sizes["yl"]
    rows = parts.shape[0]
    mine = log_sum(exchange(parts.reshape(near, rows // near, LANES), NEAR))
    mine = log_sum(spread(mine, FAR, sizes["zh"]))
    return spread(mine, NEAR, near).reshape(rows, LANES)


def over_sources(parts, sizes):
    group = sizes["yh"] * sizes["x"] * sizes["core"]
    rows = parts.shape[0]
    mine = log_sum(exchange(parts.reshape(group, rows // group, LANES), SRC))
    return spread(mine, SRC, group).reshape(rows, LANES)


def body(sizes, source, target, log_source, log_target):
    source, target = source.T, target.T
    parts, *kept, norms = first_update(target, source, log_target)
    for step in range(ITERS):
        if step:
            (parts,) = next_update(source, target, log_target, known, kept, True)
        known = over_targets(parts, sizes)
        last = step == ITERS - 1
        parts, *rest = next_update(target, source, log_source, known, kept, False, emit=last)
        known = over_sources(parts, sizes)
    tgt_potential = (known.reshape(PAIRS, -1) - norms[:1]) * BACK
    return (rest[0], tgt_potential)


def solution(mesh):
    sizes = {"yh": 2, "x": 4, "core": 2, "zh": 4, "zl": 4, "yl": 2}
    fine = Mesh(mesh.devices.reshape(tuple(sizes.values())), tuple(sizes))
    src, tgt = SRC, FAR + NEAR
    in_specs = (P(src, None), P(tgt, None), P(None, src), P(None, tgt))
    out_specs = (P(None, src), P(None, tgt))
    return jax.shard_map(
        functools.partial(body, sizes), mesh=fine, in_specs=in_specs, out_specs=out_specs, check_vma=False
    )
```

time: 215 us -> 235 us (1.093)
  the two profiles are of different devices: /device:TPU:1 before, /device:TPU:8 now
where the time goes in v2:
time: 235 us; the launch traced here: 234 us
  blocking collectives  127 us (54%)
  Pallas kernels  68.6 us (29%)
  local copies, waits for them, and re-layouts  20.2 us (9%)
  waiting for transfers between devices  12.3 us (5%)
  starting transfers between devices  3.57 us (2%)
    all_to_all x9, blocking collectives, exchange(): return lax.all_to_all(value, axes, 0, 0)  127 us
    pallas_call x3, Pallas kernels, next_update(): pl.pallas_call(functools.partial(next_kernel, to_source, emit), out_shape...  63.3 us
    unnamed x28, local copies, waits for them, and re-layouts  19.2 us
    all_to_all x1, waiting for transfers between devices, exchange(): return lax.all_to_all(value, axes, 0, 0)  12.3 us
    pallas_call x1, Pallas kernels, first_update(): pl.pallas_call(first_kernel, out_shape=[jax.ShapeDtypeStruct((PAIRS * cel...  5.31 us
  transfers between devices with their start and end apart: 1, of which 1 were waited for; matrix products, arithmetic and copies ran while one was open for 0% of the time, Pallas kernels for 0%

profile of v2, /device:TPU:8, one launch (start us, length us, event | category | flops | bytes accessed | tf_op | source)
XLA Modules:
  0.0 234.4 jit_solution(2071701505165157014)
XLA Ops:
  0.6 0.0 copy-start.4
  0.6 1.0 copy-done.4
  1.7 0.9 copy-done.7
  2.6 1.0 copy-done.10
  3.6 5.3 %shard_map.59 = (f32[256,128]{1,0:T(8,128)S(1)}, bf16[1024,4096]{1,0:T(8,128)(2,1)S(1)}, f32[8,1024]{1,0:T(8,128)S(1)}, f32[8,4096]{1,0:T(8,128)S(1)}, f32[8,4096]{1,0:T(8,128)S(1)}) custom-call(bf16[64,4096]{1,0:T(8,128)(2,1)S(1)} %bitcast.10, bf16[64,1024]{1,0:T(8,128)(2,1)S(1)} %bitcast.14, f32[32,4096]{1,0:T(8,128)S(1)} %copy-done.10), custom_call_target="tpu_custom_call" | custom-call | tf_op jit(solution)/shard_map/pallas_call | solution.py:200
  9.0 3.2 %copy-done = bf16[1024,4096]{1,0:T(8,128)(2,1)} copy-done((bf16[1024,4096]{1,0:T(8,128)(2,1)}, bf16[1024,4096]{1,0:T(8,128)(2,1)S(1)}, u32[]{:S(2)}) %copy-start) | copy-done | bytes 8388632
  12.2 13.7 %all_to_all.50 = f32[8,32,128]{2,1,0:T(8,128)S(1)} all-to-all(f32[8,32,128]{2,1,0:T(8,128)S(1)} %bitcast.24), channel_id=1, replica_groups=mesh['yh'=2,'x'=4,'core'=2,'zh'=4,'zl'=4,'yl'=2] {'zl','yl'}, dimensions={0} | all-to-all | bytes 262144 | tf_op jit(solution)/shard_map/all_to_all | solution.py:243
  26.0 24.1 %all_to_all.51 = f32[4,32,128]{2,1,0:T(8,128)S(1)} all-to-all(f32[4,32,128]{2,1,0:T(8,128)S(1)} %broadcast_in_dim.12), channel_id=1, replica_groups=mesh['yh'=2,'x'=4,'core'=2,'zh'=4,'zl'=4,'yl'=2] {'zh'}, dimensions={0} | all-to-all | bytes 131072 | tf_op jit(solution)/shard_map/all_to_all | solution.py:243
  50.2 9.7 %all_to_all.52 = f32[8,32,128]{2,1,0:T(8,128)S(1)} all-to-all(f32[8,32,128]{2,1,0:T(8,128)S(1)} %broadcast_in_dim.13), channel_id=1, replica_groups=mesh['yh'=2,'x'=4,'core'=2,'zh'=4,'zl'=4,'yl'=2] {'zl','yl'}, dimensions={0} | all-to-all | bytes 262144 | tf_op jit(solution)/shard_map/all_to_all | solution.py:243
  59.9 3.4 %copy-done.1 = bf16[1024,4096]{1,0:T(8,128)(2,1)S(1)} copy-done((bf16[1024,4096]{1,0:T(8,128)(2,1)S(1)}, bf16[1024,4096]{1,0:T(8,128)(2,1)}, u32[]{:S(2)}) %copy-start.1) | copy-done | bytes 8388632
  63.3 1.0 copy-done.5
  64.4 0.9 copy-done.8
  65.3 0.9 copy-done.12
  66.2 29.8 %shard_map.60 = f32[1024,128]{1,0:T(8,128)S(1)} custom-call(bf16[64,4096]{1,0:T(8,128)(2,1)S(1)} %bitcast.11, bf16[64,1024]{1,0:T(8,128)(2,1)S(1)} %bitcast.15, f32[32,1024]{1,0:T(8,128)S(1)} %copy-done.12, f32[256,128]{1,0:T(8,128)S(1)} %bitcast.21, bf16[1024,4096]{1,0:T(8,128)(2,1)S(1)} %copy-done.1, f32[8,1024]{1,0:T(8,128)S(1)} %get-tuple-element.11.refs_5_, ...), custom_call_target="tpu_custom_call" | custom-call | tf_op jit(solution)/shard_map/pallas_call | solution.py:224
  96.0 0.0 copy-start.13
  96.0 15.1 %all_to_all.53 = f32[16,64,128]{2,1,0:T(8,128)S(1)} all-to-all(f32[16,64,128]{2,1,0:T(8,128)S(1)} %bitcast.18), channel_id=1, replica_groups=mesh['yh'=2,'x'=4,'core'=2,'zh'=4,'zl'=4,'yl'=2] {'yh','x','core'}, dimensions={0} | all-to-all | bytes 1048576 | tf_op jit(solution)/shard_map/all_to_all | solution.py:243
  111.1 0.1 exponential_reduce_fusion.1
  111.3 15.0 %all_to_all.54 = f32[16,64,128]{2,1,0:T(8,128)S(1)} all-to-all(f32[16,64,128]{2,1,0:T(8,128)S(1)} %broadcast_in_dim.14), channel_id=1, replica_groups=mesh['yh'=2,'x'=4,'core'=2,'zh'=4,'zl'=4,'yl'=2] {'yh','x','core'}, dimensions={0} | all-to-all | bytes 1048576 | tf_op jit(solution)/shard_map/all_to_all | solution.py:243
  126.3 3.4 %copy-done.2 = bf16[1024,4096]{1,0:T(8,128)(2,1)S(1)} copy-done((bf16[1024,4096]{1,0:T(8,128)(2,1)S(1)}, bf16[1024,4096]{1,0:T(8,128)(2,1)}, u32[]{:S(2)}) %copy-start.2) | copy-done | bytes 8388632
  129.7 3.1 %shard_map.61 = f32[256,128]{1,0:T(8,128)S(1)} custom-call(bf16[64,1024]{1,0:T(8,128)(2,1)S(1)} %bitcast.16, bf16[64,4096]{1,0:T(8,128)(2,1)S(1)} %bitcast.12, f32[32,4096]{1,0:T(8,128)S(1)} %copy-done.11, f32[1024,128]{1,0:T(8,128)S(1)} %bitcast.19, bf16[1024,4096]{1,0:T(8,128)(2,1)S(1)} %copy-done.2, f32[8,1024]{1,0:T(8,128)S(1)} %get-tuple-element.11.refs_5_, ...), custom_call_target="tpu_custom_call" | custom-call | tf_op jit(solution)/shard_map/pallas_call | solution.py:224
  132.8 8.6 %all_to_all.55 = f32[8,32,128]{2,1,0:T(8,128)S(1)} all-to-all(f32[8,32,128]{2,1,0:T(8,128)S(1)} %bitcast.22), channel_id=1, replica_groups=mesh['yh'=2,'x'=4,'core'=2,'zh'=4,'zl'=4,'yl'=2] {'zl','yl'}, dimensions={0} | all-to-all | bytes 262144 | tf_op jit(solution)/shard_map/all_to_all | solution.py:243
  141.5 16.2 %all_to_all.56 = f32[4,32,128]{2,1,0:T(8,128)S(1)} all-to-all(f32[4,32,128]{2,1,0:T(8,128)S(1)} %broadcast_in_dim.15), channel_id=1, replica_groups=mesh['yh'=2,'x'=4,'core'=2,'zh'=4,'zl'=4,'yl'=2] {'zh'}, dimensions={0} | all-to-all | bytes 131072 | tf_op jit(solution)/shard_map/all_to_all | solution.py:243
  157.9 9.9 %all_to_all.57 = f32[8,32,128]{2,1,0:T(8,128)S(1)} all-to-all(f32[8,32,128]{2,1,0:T(8,128)S(1)} %broadcast_in_dim.16), channel_id=1, replica_groups=mesh['yh'=2,'x'=4,'core'=2,'zh'=4,'zl'=4,'yl'=2] {'zl','yl'}, dimensions={0} | all-to-all | bytes 262144 | tf_op jit(solution)/shard_map/all_to_all | solution.py:243
  167.7 3.4 %copy-done.3 = bf16[1024,4096]{1,0:T(8,128)(2,1)S(1)} copy-done((bf16[1024,4096]{1,0:T(8,128)(2,1)S(1)}, bf16[1024,4096]{1,0:T(8,128)(2,1)}, u32[]{:S(2)}) %copy-start.3) | copy-done | bytes 8388632
  171.1 30.3 %shard_map.62 = (f32[1024,128]{1,0:T(8,128)S(1)}, f32[32,1024]{1,0:T(8,128)}) custom-call(bf16[64,4096]{1,0:T(8,128)(2,1)S(1)} %bitcast.13, bf16[64,1024]{1,0:T(8,128)(2,1)S(1)} %bitcast.17, f32[32,1024]{1,0:T(8,128)S(1)} %copy-done.13, f32[256,128]{1,0:T(8,128)S(1)} %bitcast.20, bf16[1024,4096]{1,0:T(8,128)(2,1)S(1)} %copy-done.3, ...), custom_call_target="tpu_custom_call" | custom-call | tf_op jit(solution)/shard_map/pallas_call | solution.py:224
  201.5 15.0 %all_to_all.58 = f32[16,64,128]{2,1,0:T(8,128)S(1)} all-to-all(f32[16,64,128]{2,1,0:T(8,128)S(1)} %bitcast.23), channel_id=1, replica_groups=mesh['yh'=2,'x'=4,'core'=2,'zh'=4,'zl'=4,'yl'=2] {'yh','x','core'}, dimensions={0} | all-to-all | bytes 1048576 | tf_op jit(solution)/shard_map/all_to_all | solution.py:243
  216.5 0.1 exponential_reduce_fusion
  216.7 0.8 broadcast_in_dim.17
  217.5 3.6 %all-to-all-start.9 = ((f32[16,64,128]{2,1,0:T(8,128)}), f32[16,64,128]{2,1,0:T(8,128)S(1)}, u32[]{:S(2)}, u32[]{:S(2)}) async-start(f32[16,64,128]{2,1,0:T(8,128)} %broadcast_in_dim.17), calls=%async_computation.9 | async-start | bytes 1048576 | tf_op jit(solution)/shard_map/all_to_all | solution.py:243
  221.1 12.3 %all-to-all-done.9 = f32[16,64,128]{2,1,0:T(8,128)S(1)} async-done(((f32[16,64,128]{2,1,0:T(8,128)}), f32[16,64,128]{2,1,0:T(8,128)S(1)}, u32[]{:S(2)}, u32[]{:S(2)}) %all-to-all-start.9) | async-done | bytes 524320 | tf_op jit(solution)/shard_map/all_to_all | solution.py:243
  233.4 0.1 reshape_reshape.3
  233.5 0.8 subtract_multiply_fusion
  (38 shorter events, 0.4 us)
Async XLA Ops:
  0.6 1.0 copy-start.4
  1.7 0.9 copy-start.7
  2.6 1.0 copy-start.10
  3.6 122.7 %copy-start.6 = (bf16[4096,64]{0,1:T(8,128)(2,1)S(1)}, bf16[4096,64]{0,1:T(8,128)(2,1)}, u32[]{:S(2)}) copy-start(bf16[4096,64]{0,1:T(8,128)(2,1)} %param.5) | copy-start | bytes 1572868
  3.6 122.7 %copy-start.9 = (bf16[1024,64]{0,1:T(8,128)(2,1)S(1)}, bf16[1024,64]{0,1:T(8,128)(2,1)}, u32[]{:S(2)}) copy-start(bf16[1024,64]{0,1:T(8,128)(2,1)} %param.4) | copy-start | bytes 393220
  3.6 122.7 %copy-start.11 = (f32[32,4096]{1,0:T(8,128)S(1)}, f32[32,4096]{1,0:T(8,128)}, u32[]{:S(2)}) copy-start(f32[32,4096]{1,0:T(8,128)} %refs_2_.4) | copy-start | bytes 1572868
  8.9 3.2 %copy-start = (bf16[1024,4096]{1,0:T(8,128)(2,1)}, bf16[1024,4096]{1,0:T(8,128)(2,1)S(1)}, u32[]{:S(2)}) copy-start(bf16[1024,4096]{1,0:T(8,128)(2,1)S(1)} %get-tuple-element.10.refs_4_) | copy-start | bytes 25165828
  59.9 3.4 %copy-start.1 = (bf16[1024,4096]{1,0:T(8,128)(2,1)S(1)}, bf16[1024,4096]{1,0:T(8,128)(2,1)}, u32[]{:S(2)}) copy-start(bf16[1024,4096]{1,0:T(8,128)(2,1)} %copy-done) | copy-start | bytes 25165828
  63.3 1.0 copy-start.5
  64.4 0.9 copy-start.8
  65.3 0.9 copy-start.12
  96.0 71.8 %copy-start.13 = (f32[32,1024]{1,0:T(8,128)S(1)}, f32[32,1024]{1,0:T(8,128)}, u32[]{:S(2)}) copy-start(f32[32,1024]{1,0:T(8,128)} %refs_2_.5) | copy-start | bytes 393220
  126.3 3.4 %copy-start.2 = (bf16[1024,4096]{1,0:T(8,128)(2,1)S(1)}, bf16[1024,4096]{1,0:T(8,128)(2,1)}, u32[]{:S(2)}) copy-start(bf16[1024,4096]{1,0:T(8,128)(2,1)} %copy-done) | copy-start | bytes 25165828
  167.7 3.4 %copy-start.3 = (bf16[1024,4096]{1,0:T(8,128)(2,1)S(1)}, bf16[1024,4096]{1,0:T(8,128)(2,1)}, u32[]{:S(2)}) copy-start(bf16[1024,4096]{1,0:T(8,128)(2,1)} %copy-done) | copy-start | bytes 25165828
  217.5 15.9 %all-to-all-start.9 = ((f32[16,64,128]{2,1,0:T(8,128)}), f32[16,64,128]{2,1,0:T(8,128)S(1)}, u32[]{:S(2)}, u32[]{:S(2)}) async-start(f32[16,64,128]{2,1,0:T(8,128)} %broadcast_in_dim.17), calls=%async_computation.9 | async-start | bytes 1048576 | tf_op jit(solution)/shard_map/all_to_all | solution.py:243

commit v3 on v2

--- a/solution.py
+++ b/solution.py
@@ -71,15 +71,32 @@
     return jnp.broadcast_to(column, (rows, LANES)).T[:1]
 
 
-def first_kernel(target_ref, source_ref, log_ref, out_ref, kept_ref, peak_ref, bias_ref, norm_ref,
-                 left_ref, right_ref, weight_ref, shift_ref):
+def arrive(pairs, sems):
+    copies = [pltpu.make_async_copy(src, dst, sems.at[k]) for k, (src, dst) in enumerate(pairs)]
+    for copy in copies:
+        copy.start()
+    return copies
+
+
+def first_kernel(target_hbm, source_hbm, log_target_hbm, log_source_hbm,
+                 out_ref, kept_ref, peak_ref, bias_ref, target_norm_ref, source_norm_ref, log_target_ref,
+                 log_source_ref, target_ref, source_ref, left_ref, right_ref, weight_ref, shift_ref, sems):
     cells, others = kept_ref.shape
+    copies = arrive(
+        [(source_hbm, source_ref), (log_target_hbm, log_target_ref), (target_hbm, target_ref),
+         (log_source_hbm, log_source_ref)],
+        sems,
+    )
+    copies[0].wait()
     fill_left(left_ref, source_ref)
-    norms = half_norms(target_ref[...])
-    norm_ref[...] = jnp.broadcast_to(norms, norm_ref.shape)
-    pot = log_ref[...] * LOG2E
+    source_norm_ref[...] = jnp.broadcast_to(half_norms(source_ref[...]), source_norm_ref.shape)
+    copies[1].wait()
+    pot = log_target_ref[...] * LOG2E
     top = jnp.max(pot, axis=0, keepdims=True)
     weight_ref[...] = jnp.exp2(pot - top).astype(jnp.bfloat16)
+    copies[2].wait()
+    norms = half_norms(target_ref[...])
+    target_norm_ref[...] = jnp.broadcast_to(norms, target_norm_ref.shape)
     bias = top - norms
     bias_ref[...] = jnp.broadcast_to(bias, bias_ref.shape)
     fill_right(right_ref, target_ref, bias)
@@ -115,6 +132,7 @@
             result = row + jnp.log2(total[:, k * LANES : (k + 1) * LANES])
             out_ref[pl.ds(tile * (TILE // LANES) + k, PAIRS, stride=cells // LANES), :] = result
         peak = after
+    copies[3].wait()
 
 
 def again(out_ref, cells_ref, others_ref, pot_ref, left_ref, right_ref, weight_ref):
@@ -155,19 +173,20 @@
 
 def next_kernel(to_source, emit, *refs):
     refs = list(refs)
-    cells_ref, others_ref, log_ref, known_ref, kept_ref, peak_ref, bias_ref, out_ref = refs[:8]
-    refs = refs[8:]
+    cells_hbm, others_hbm, log_ref, known_ref, kept_ref, peak_ref, bias_ref = refs[:7]
+    refs = refs[7:]
+    norm_ref = refs.pop(0) if emit else None
+    out_ref = refs.pop(0)
     pot_out = refs.pop(0) if emit else None
-    pot_ref, left_ref, right_ref, weight_ref = refs
+    cells_ref, others_ref, pot_ref, left_ref, right_ref, weight_ref, sems = refs
     cells, others = left_ref.shape[0], right_ref.shape[1]
 
     log_sums_of(known_ref, log_ref, pot_ref)
     if emit:
-        norms = half_norms(others_ref[...])
         rows = others // LANES
         for row in range(rows):
             part = slice(row * LANES, (row + 1) * LANES)
-            pot_out[:, part] = (known_ref[pl.ds(row, PAIRS, stride=rows), :] - norms[:, part]) * BACK
+            pot_out[:, part] = (known_ref[pl.ds(row, PAIRS, stride=rows), :] - norm_ref[:1, part]) * BACK
     pot = pot_ref[...]
     scaled = pot - bias_ref[:1] if to_source else pot + peak_ref[:1]
     most = jnp.max(jnp.max(scaled, axis=0, keepdims=True), axis=1, keepdims=True)
@@ -189,13 +208,21 @@
 
     @pl.when(jnp.logical_not(least >= SMALL))
     def _():
+        for copy in arrive([(cells_hbm, cells_ref), (others_hbm, others_ref)], sems):
+            copy.wait()
         again(out_ref, cells_ref, others_ref, pot_ref, left_ref, right_ref, weight_ref)
 
 
-LIMIT = pltpu.CompilerParams(vmem_limit_bytes=28 * 1024 * 1024)
-
-
-def first_update(target, source, log):
+LIMIT = pltpu.CompilerParams(vmem_limit_bytes=24 * 1024 * 1024)
+HBM = pl.BlockSpec(memory_space=pltpu.HBM)
+VMEM = pl.BlockSpec(memory_space=pltpu.VMEM)
+
+
+def in_hbm(*arrays):
+    return [pltpu.with_memory_space_constraint(array, pltpu.HBM) for array in arrays]
+
+
+def first_update(target, source, log_target, log_source):
     others, cells = target.shape[1], source.shape[1]
     return pl.pallas_call(
         first_kernel,
@@ -205,33 +232,49 @@
             jax.ShapeDtypeStruct((8, cells), jnp.float32),
             jax.ShapeDtypeStruct((8, others), jnp.float32),
             jax.ShapeDtypeStruct((8, others), jnp.float32),
+            jax.ShapeDtypeStruct((8, cells), jnp.float32),
+            jax.ShapeDtypeStruct(log_target.shape, log_target.dtype),
+            jax.ShapeDtypeStruct(log_source.shape, log_source.dtype),
         ],
+        in_specs=[HBM] * 4,
+        out_specs=[VMEM] * 8,
         scratch_shapes=[
+            pltpu.VMEM(target.shape, target.dtype),
+            pltpu.VMEM(source.shape, source.dtype),
             pltpu.VMEM((cells, DEPTH), jnp.bfloat16),
             pltpu.VMEM((DEPTH, others), jnp.bfloat16),
             pltpu.VMEM((PAIRS, others), jnp.bfloat16),
             pltpu.VMEM((2, TILE, others), jnp.float32),
+            pltpu.SemaphoreType.DMA((4,)),
         ],
         compiler_params=LIMIT,
-    )(target, source, log)
-
-
-def next_update(cells, others, log, known, kept, to_source, emit=False):
+    )(*in_hbm(target, source, log_target, log_source))
+
+
+def next_update(cells, others, log, known, kept, to_source, norms=None):
     own, count = cells.shape[1], others.shape[1]
+    emit = norms is not None
     out = [jax.ShapeDtypeStruct((PAIRS * own // LANES, LANES), jnp.float32)]
+    args = [*in_hbm(cells, others), log, known, *kept]
     if emit:
         out.append(jax.ShapeDtypeStruct((PAIRS, count), jnp.float32))
+        args.append(norms)
     return pl.pallas_call(
         functools.partial(next_kernel, to_source, emit),
         out_shape=out,
+        in_specs=[HBM] * 2 + [VMEM] * (len(args) - 2),
+        out_specs=[VMEM] * len(out),
         scratch_shapes=[
+            pltpu.VMEM(cells.shape, cells.dtype),
+            pltpu.VMEM(others.shape, others.dtype),
             pltpu.VMEM((PAIRS, count), jnp.float32),
             pltpu.VMEM((own, DEPTH), jnp.bfloat16),
             pltpu.VMEM((DEPTH, count), jnp.bfloat16),
             pltpu.VMEM((PAIRS, count), jnp.bfloat16),
+            pltpu.SemaphoreType.DMA((2,)),
         ],
         compiler_params=LIMIT,
-    )(cells, others, log, known, *kept)
+    )(*args)
 
 
 def log_sum(parts):
@@ -239,41 +282,65 @@
     return best + jnp.log2(jnp.sum(jnp.exp2(parts - best[None]), axis=0))
 
 
+def combine_kernel(parts_ref, out_ref):
+    out_ref[...] = jnp.broadcast_to(log_sum(parts_ref[...])[None], out_ref.shape)
+
+
+def combine(parts, copies):
+    return pl.pallas_call(
+        combine_kernel,
+        out_shape=jax.ShapeDtypeStruct((copies,) + parts.shape[1:], jnp.float32),
+        compiler_params=pltpu.CompilerParams(vmem_limit_bytes=4 * 1024 * 1024),
+    )(parts)
+
+
+def finish_kernel(known_ref, norm_ref, out_ref):
+    rows = out_ref.shape[1] // LANES
+    for row in range(rows):
+        part = slice(row * LANES, (row + 1) * LANES)
+        out_ref[:, part] = (known_ref[pl.ds(row, PAIRS, stride=rows), :] - norm_ref[:1, part]) * BACK
+
+
+def finish(known, norms):
+    return pl.pallas_call(
+        finish_kernel,
+        out_shape=jax.ShapeDtypeStruct((PAIRS, norms.shape[1]), jnp.float32),
+        compiler_params=pltpu.CompilerParams(vmem_limit_bytes=4 * 1024 * 1024),
+    )(known, norms)
+
+
 def exchange(value, axes):
     return lax.all_to_all(value, axes, 0, 0)
-
-
-def spread(value, axes, count):
-    return exchange(jnp.broadcast_to(value[None], (count,) + value.shape), axes)
 
 
 def over_targets(parts, sizes):
     near = sizes["zl"] * sizes["yl"]
     rows = parts.shape[0]
-    mine = log_sum(exchange(parts.reshape(near, rows // near, LANES), NEAR))
-    mine = log_sum(spread(mine, FAR, sizes["zh"]))
-    return spread(mine, NEAR, near).reshape(rows, LANES)
+    mine = exchange(parts.reshape(near, rows // near, LANES), NEAR)
+    mine = exchange(combine(mine, sizes["zh"]), FAR)
+    return exchange(combine(mine, near), NEAR).reshape(rows, LANES)
 
 
 def over_sources(parts, sizes):
     group = sizes["yh"] * sizes["x"] * sizes["core"]
     rows = parts.shape[0]
-    mine = log_sum(exchange(parts.reshape(group, rows // group, LANES), SRC))
-    return spread(mine, SRC, group).reshape(rows, LANES)
+    mine = exchange(parts.reshape(group, rows // group, LANES), SRC)
+    return exchange(combine(mine, group), SRC).reshape(rows, LANES)
 
 
 def body(sizes, source, target, log_source, log_target):
     source, target = source.T, target.T
-    parts, *kept, norms = first_update(target, source, log_target)
+    parts, *kept, target_norms, source_norms, log_target, log_source = first_update(
+        target, source, log_target, log_source
+    )
     for step in range(ITERS):
         if step:
             (parts,) = next_update(source, target, log_target, known, kept, True)
         known = over_targets(parts, sizes)
-        last = step == ITERS - 1
-        parts, *rest = next_update(target, source, log_source, known, kept, False, emit=last)
+        norms = source_norms if step == ITERS - 1 else None
+        parts, *rest = next_update(target, source, log_source, known, kept, False, norms)
         known = over_sources(parts, sizes)
-    tgt_potential = (known.reshape(PAIRS, -1) - norms[:1]) * BACK
-    return (rest[0], tgt_potential)
+    return (rest[0], finish(known, target_norms))
 
 
 def solution(mesh):

time: 235 us -> 182 us (0.77)
  the two profiles are of different devices: /device:TPU:8 before, /device:TPU:200 now
where the time goes in v3:
time: 182 us; the launch traced here: 181 us
  blocking collectives  165 us (91%)
  Pallas kernels  15.8 us (9%)
    all_to_all x10, blocking collectives, exchange(): return lax.all_to_all(value, axes, 0, 0)  165 us
    pallas_call x3, Pallas kernels, next_update(): pl.pallas_call(functools.partial(next_kernel, to_source, emit), out_shape...  7.79 us
    pallas_call x1, Pallas kernels, first_update(): pl.pallas_call(first_kernel, out_shape=[jax.ShapeDtypeStruct((PAIRS * cel...  6.53 us

profile of v3, /device:TPU:200, one launch (start us, length us, event | category | flops | bytes accessed | tf_op | source)
XLA Modules:
  0.0 181.1 jit_solution(16753591221593691574)
XLA Ops:
  0.6 6.5 %shard_map.59 = (f32[256,128]{1,0:T(8,128)S(1)}, bf16[1024,4096]{1,0:T(8,128)(2,1)S(1)}, f32[8,1024]{1,0:T(8,128)S(1)}, f32[8,4096]{1,0:T(8,128)S(1)}, f32[8,409...) custom-call(bf16[64,4096]{1,0:T(8,128)(2,1)} %bitcast.18, ...), custom_call_target="tpu_custom_call" | custom-call | tf_op jit(solution)/shard_map/pallas_call | solution.py:227
  7.2 9.8 %all_to_all.50.parts_ref = f32[8,32,128]{2,1,0:T(8,128)S(1)} all-to-all(f32[8,32,128]{2,1,0:T(8,128)S(1)} %bitcast.17), channel_id=1, replica_groups=mesh['yh'=2,'x'=4,'core'=2,'zh'=4,'zl'=4,'yl'=2] {'zl','yl'}, dimensions={0} | all-to-all | bytes 262144 | tf_op jit(solution)/shard_map/all_to_all | solution.py:313
  17.0 18.4 %all_to_all.51.parts_ref = f32[4,32,128]{2,1,0:T(8,128)S(1)} all-to-all(f32[4,32,128]{2,1,0:T(8,128)S(1)} %shard_map.60), channel_id=1, replica_groups=mesh['yh'=2,'x'=4,'core'=2,'zh'=4,'zl'=4,'yl'=2] {'zh'}, dimensions={0} | all-to-all | bytes 131072 | tf_op jit(solution)/shard_map/all_to_all | solution.py:313
  35.5 9.9 %all_to_all.52 = f32[8,32,128]{2,1,0:T(8,128)S(1)} all-to-all(f32[8,32,128]{2,1,0:T(8,128)S(1)} %shard_map.61), channel_id=1, replica_groups=mesh['yh'=2,'x'=4,'core'=2,'zh'=4,'zl'=4,'yl'=2] {'zl','yl'}, dimensions={0} | all-to-all | bytes 262144 | tf_op jit(solution)/shard_map/all_to_all | solution.py:313
  45.4 2.0 %shard_map.62 = f32[1024,128]{1,0:T(8,128)S(1)} custom-call(bf16[64,4096]{1,0:T(8,128)(2,1)} %bitcast.19, bf16[64,1024]{1,0:T(8,128)(2,1)} %bitcast.23, f32[32,1024]{1,0:T(8,128)S(1)} %get-tuple-element.12.refs_2_, f32[256,128]{1,0:T(8,128)S(1)} %bitcast.15, bf16[1024,4096]{1,0:T(8,128)(2,1)S(1)} %get-tuple-element.15.refs_4_, ...), custom_call_target="tpu_custom_call" | custom-call | tf_op jit(solution)/shard_map/pallas_call | solution.py:262
  47.4 18.3 %all_to_all.53.parts_ref = f32[16,64,128]{2,1,0:T(8,128)S(1)} all-to-all(f32[16,64,128]{2,1,0:T(8,128)S(1)} %bitcast.11), channel_id=1, replica_groups=mesh['yh'=2,'x'=4,'core'=2,'zh'=4,'zl'=4,'yl'=2] {'yh','x','core'}, dimensions={0} | all-to-all | bytes 1048576 | tf_op jit(solution)/shard_map/all_to_all | solution.py:313
  65.7 0.1 shard_map.63
  65.8 15.0 %all_to_all.54 = f32[16,64,128]{2,1,0:T(8,128)S(1)} all-to-all(f32[16,64,128]{2,1,0:T(8,128)S(1)} %shard_map.63), channel_id=1, replica_groups=mesh['yh'=2,'x'=4,'core'=2,'zh'=4,'zl'=4,'yl'=2] {'yh','x','core'}, dimensions={0} | all-to-all | bytes 1048576 | tf_op jit(solution)/shard_map/all_to_all | solution.py:313
  80.8 3.1 %shard_map.64 = f32[256,128]{1,0:T(8,128)S(1)} custom-call(bf16[64,1024]{1,0:T(8,128)(2,1)} %bitcast.24, bf16[64,4096]{1,0:T(8,128)(2,1)} %bitcast.20, f32[32,4096]{1,0:T(8,128)S(1)} %get-tuple-element.13.refs_2_, f32[1024,128]{1,0:T(8,128)S(1)} %bitcast.10, bf16[1024,4096]{1,0:T(8,128)(2,1)S(1)} %get-tuple-element.15.refs_4_, ...), custom_call_target="tpu_custom_call" | custom-call | tf_op jit(solution)/shard_map/pallas_call | solution.py:262
  83.9 10.3 %all_to_all.55.parts_ref = f32[8,32,128]{2,1,0:T(8,128)S(1)} all-to-all(f32[8,32,128]{2,1,0:T(8,128)S(1)} %bitcast.14), channel_id=1, replica_groups=mesh['yh'=2,'x'=4,'core'=2,'zh'=4,'zl'=4,'yl'=2] {'zl','yl'}, dimensions={0} | all-to-all | bytes 262144 | tf_op jit(solution)/shard_map/all_to_all | solution.py:313
  94.3 15.2 %all_to_all.56.parts_ref = f32[4,32,128]{2,1,0:T(8,128)S(1)} all-to-all(f32[4,32,128]{2,1,0:T(8,128)S(1)} %shard_map.65), channel_id=1, replica_groups=mesh['yh'=2,'x'=4,'core'=2,'zh'=4,'zl'=4,'yl'=2] {'zh'}, dimensions={0} | all-to-all | bytes 131072 | tf_op jit(solution)/shard_map/all_to_all | solution.py:313
  109.6 9.9 %all_to_all.57 = f32[8,32,128]{2,1,0:T(8,128)S(1)} all-to-all(f32[8,32,128]{2,1,0:T(8,128)S(1)} %shard_map.66), channel_id=1, replica_groups=mesh['yh'=2,'x'=4,'core'=2,'zh'=4,'zl'=4,'yl'=2] {'zl','yl'}, dimensions={0} | all-to-all | bytes 262144 | tf_op jit(solution)/shard_map/all_to_all | solution.py:313
  119.5 2.6 %shard_map.67 = (f32[1024,128]{1,0:T(8,128)S(1)}, f32[32,1024]{1,0:T(8,128)}) custom-call(bf16[64,4096]{1,0:T(8,128)(2,1)} %bitcast.21, bf16[64,1024]{1,0:T(8,128)(2,1)} %bitcast.25, f32[32,1024]{1,0:T(8,128)S(1)} %get-tuple-element.12.refs_2_, f32[256,128]{1,0:T(8,128)S(1)} %bitcast.13, bf16[1024,4096]{1,0:T(8,128)(2,1)S(1)} %get-tuple-element.15.refs_4_, ...), custom_call_target="tpu_custom_call" | custom-call | tf_op jit(solution)/shard_map/pallas_call | solution.py:262
  122.1 42.7 %all_to_all.58.parts_ref = f32[16,64,128]{2,1,0:T(8,128)S(1)} all-to-all(f32[16,64,128]{2,1,0:T(8,128)S(1)} %bitcast.16), channel_id=1, replica_groups=mesh['yh'=2,'x'=4,'core'=2,'zh'=4,'zl'=4,'yl'=2] {'yh','x','core'}, dimensions={0} | all-to-all | bytes 1048576 | tf_op jit(solution)/shard_map/all_to_all | solution.py:313
  164.8 0.1 shard_map.68
  165.0 15.0 %all_to_all.59 = f32[16,64,128]{2,1,0:T(8,128)S(1)} all-to-all(f32[16,64,128]{2,1,0:T(8,128)S(1)} %shard_map.68), channel_id=1, replica_groups=mesh['yh'=2,'x'=4,'core'=2,'zh'=4,'zl'=4,'yl'=2] {'yh','x','core'}, dimensions={0} | all-to-all | bytes 1048576 | tf_op jit(solution)/shard_map/all_to_all | solution.py:313
  179.9 1.1 shard_map.69
  (4 shorter events, 0.1 us)

commit v4 on v3

--- a/solution.py
+++ b/solution.py
@@ -13,6 +13,7 @@
 ITERS = 2
 PAIRS = 32
 LANES = 128
+GROUP = 8
 DEPTH = 256
 
 entropy = 0.1
@@ -25,7 +26,8 @@
 
 NEAR = ("zl", "yl")
 FAR = ("zh",)
-SRC = ("yh", "x", "core")
+CHIPS = ("yh", "x")
+SRC = CHIPS + ("core",)
 
 TILE = 256
 CHUNK = 512
@@ -64,6 +66,10 @@
     block = jnp.where(row == 0, high, jnp.where(row == 1, middle, jnp.where(row == 2, low, 0.0)))
     right_ref[3 * FEAT : 3 * FEAT + 16, :] = block.astype(jnp.bfloat16)
     right_ref[3 * FEAT + 16 :, :] = jnp.zeros((DEPTH - 3 * FEAT - 16, count), jnp.bfloat16)
+
+
+def tile_rows(group, column, count):
+    return slice((group * (count // LANES) + column) * GROUP, (group * (count // LANES) + column + 1) * GROUP)
 
 
 def as_row(column):
@@ -127,17 +133,20 @@
             total = sums if total is None else total + sums
         for k in range(TILE // LANES):
             part = slice(tile * TILE + k * LANES, tile * TILE + (k + 1) * LANES)
-            row = as_row(peak[k * LANES : (k + 1) * LANES])
-            peak_ref[:, part] = jnp.broadcast_to(row, (8, LANES))
-            result = row + jnp.log2(total[:, k * LANES : (k + 1) * LANES])
-            out_ref[pl.ds(tile * (TILE // LANES) + k, PAIRS, stride=cells // LANES), :] = result
+            row = jnp.broadcast_to(as_row(peak[k * LANES : (k + 1) * LANES]), (GROUP, LANES))
+            peak_ref[:, part] = row
+            result = jnp.log2(total[:, k * LANES : (k + 1) * LANES])
+            for group in range(PAIRS // GROUP):
+                place = tile_rows(group, tile * (TILE // LANES) + k, cells)
+                out_ref[place, :] = row + result[group * GROUP : (group + 1) * GROUP]
         peak = after
     copies[3].wait()
 
 
-def again(out_ref, cells_ref, others_ref, pot_ref, left_ref, right_ref, weight_ref):
+def again(put, cells_ref, others_ref, log_ref, known_ref, pot_ref, left_ref, right_ref, weight_ref):
     cells, others = left_ref.shape[0], right_ref.shape[1]
     fill_left(left_ref, cells_ref)
+    potentials(log_ref, known_ref, pot_ref)
     pot = pot_ref[...]
     top = jnp.max(pot, axis=0, keepdims=True)
     weight_ref[...] = jnp.exp2(pot - top).astype(jnp.bfloat16)
@@ -158,39 +167,53 @@
 
         start = (jnp.full((LANES, LANES), -jnp.inf, jnp.float32), jnp.zeros((PAIRS, LANES), jnp.float32))
         peak, total = lax.fori_loop(0, others // CHUNK, chunk, start)
-        out_ref[pl.ds(index, PAIRS, stride=cells // LANES), :] = peak.T[:1] + jnp.log2(total)
+        put(index, peak.T[:1] + jnp.log2(total))
         return carry
 
     lax.fori_loop(0, cells // LANES, tile, 0)
 
 
-def log_sums_of(known_ref, log_ref, pot_ref):
-    rows = log_ref.shape[1] // LANES
-    for row in range(rows):
-        part = slice(row * LANES, (row + 1) * LANES)
-        pot_ref[:, part] = log_ref[:, part] * LOG2E - known_ref[pl.ds(row, PAIRS, stride=rows), :]
-
-
-def next_kernel(to_source, emit, *refs):
-    refs = list(refs)
+def potentials(log_ref, known_ref, pot_ref, add=None):
+    count = log_ref.shape[1]
+    most = None
+    for column in range(count // LANES):
+        part = slice(column * LANES, (column + 1) * LANES)
+        row = 0.0 if add is None else add(part)
+        for group in range(PAIRS // GROUP):
+            pairs = slice(group * GROUP, (group + 1) * GROUP)
+            value = log_ref[pairs, part] * LOG2E - known_ref[tile_rows(group, column, count), :] + row
+            pot_ref[pairs, part] = value
+            most = value if most is None else jnp.maximum(most, value)
+    return jnp.max(jnp.max(most, axis=0, keepdims=True), axis=1, keepdims=True)
+
+
+def next_kernel(to_source, *refs):
     cells_hbm, others_hbm, log_ref, known_ref, kept_ref, peak_ref, bias_ref = refs[:7]
-    refs = refs[7:]
-    norm_ref = refs.pop(0) if emit else None
-    out_ref = refs.pop(0)
-    pot_out = refs.pop(0) if emit else None
-    cells_ref, others_ref, pot_ref, left_ref, right_ref, weight_ref, sems = refs
+    outs = refs[7:8] if to_source else refs[7:9]
+    cells_ref, others_ref, pot_ref, left_ref, right_ref, weight_ref, sems = refs[7 + len(outs) :]
     cells, others = left_ref.shape[0], right_ref.shape[1]
-
-    log_sums_of(known_ref, log_ref, pot_ref)
-    if emit:
-        rows = others // LANES
-        for row in range(rows):
-            part = slice(row * LANES, (row + 1) * LANES)
-            pot_out[:, part] = (known_ref[pl.ds(row, PAIRS, stride=rows), :] - norm_ref[:1, part]) * BACK
-    pot = pot_ref[...]
-    scaled = pot - bias_ref[:1] if to_source else pot + peak_ref[:1]
-    most = jnp.max(jnp.max(scaled, axis=0, keepdims=True), axis=1, keepdims=True)
-    weight_ref[...] = jnp.exp2(scaled - most).astype(jnp.bfloat16)
+    groups = PAIRS // GROUP
+
+    if to_source:
+        most = potentials(log_ref, known_ref, pot_ref, lambda part: -bias_ref[:, part])
+
+        def put(column, result):
+            for group in range(groups):
+                place = pl.ds((group * (cells // LANES) + column) * GROUP, GROUP)
+                outs[0][place, :] = result[group * GROUP : (group + 1) * GROUP]
+    else:
+        most = potentials(log_ref, known_ref, pot_ref, lambda part: peak_ref[:, part])
+        lower = lax.axis_index("core") == 0
+
+        def put(column, result):
+            for group in range(groups // 2):
+                place = pl.ds((group * (cells // LANES) + column) * GROUP, GROUP)
+                low = result[group * GROUP : (group + 1) * GROUP]
+                high = result[(group + groups // 2) * GROUP : (group + groups // 2 + 1) * GROUP]
+                outs[0][place, :] = jnp.where(lower, low, high)
+                outs[1][place, :] = jnp.where(lower, high, low)
+
+    weight_ref[...] = jnp.exp2(pot_ref[...] - most).astype(jnp.bfloat16)
     least = None
     for at in range(0, cells, TILE):
         if to_source:
@@ -202,15 +225,14 @@
         for k in range(TILE // LANES):
             part = slice(at + k * LANES, at + (k + 1) * LANES)
             back = peak_ref[:1, part] if to_source else -bias_ref[:1, part]
-            result = (back + most) + jnp.log2(total[:, k * LANES : (k + 1) * LANES])
-            out_ref[pl.ds(part.start // LANES, PAIRS, stride=cells // LANES), :] = result
+            put(part.start // LANES, (back + most) + jnp.log2(total[:, k * LANES : (k + 1) * LANES]))
     least = jnp.min(least)
 
     @pl.when(jnp.logical_not(least >= SMALL))
     def _():
         for copy in arrive([(cells_hbm, cells_ref), (others_hbm, others_ref)], sems):
             copy.wait()
-        again(out_ref, cells_ref, others_ref, pot_ref, left_ref, right_ref, weight_ref)
+        again(put, cells_ref, others_ref, log_ref, known_ref, pot_ref, left_ref, right_ref, weight_ref)
 
 
 LIMIT = pltpu.CompilerParams(vmem_limit_bytes=24 * 1024 * 1024)
@@ -251,19 +273,14 @@
     )(*in_hbm(target, source, log_target, log_source))
 
 
-def next_update(cells, others, log, known, kept, to_source, norms=None):
+def next_update(cells, others, log, known, kept, to_source):
     own, count = cells.shape[1], others.shape[1]
-    emit = norms is not None
-    out = [jax.ShapeDtypeStruct((PAIRS * own // LANES, LANES), jnp.float32)]
-    args = [*in_hbm(cells, others), log, known, *kept]
-    if emit:
-        out.append(jax.ShapeDtypeStruct((PAIRS, count), jnp.float32))
-        args.append(norms)
+    halves = 1 if to_source else 2
     return pl.pallas_call(
-        functools.partial(next_kernel, to_source, emit),
-        out_shape=out,
-        in_specs=[HBM] * 2 + [VMEM] * (len(args) - 2),
-        out_specs=[VMEM] * len(out),
+        functools.partial(next_kernel, to_source),
+        out_shape=[jax.ShapeDtypeStruct((PAIRS * own // LANES // halves, LANES), jnp.float32)] * halves,
+        in_specs=[HBM] * 2 + [VMEM] * (2 + len(kept)),
+        out_specs=[VMEM] * halves,
         scratch_shapes=[
             pltpu.VMEM(cells.shape, cells.dtype),
             pltpu.VMEM(others.shape, others.dtype),
@@ -274,7 +291,7 @@
             pltpu.SemaphoreType.DMA((2,)),
         ],
         compiler_params=LIMIT,
-    )(*args)
+    )(*in_hbm(cells, others), log, known, *kept)
 
 
 def log_sum(parts):
@@ -294,19 +311,50 @@
     )(parts)
 
 
-def finish_kernel(known_ref, norm_ref, out_ref):
-    rows = out_ref.shape[1] // LANES
-    for row in range(rows):
-        part = slice(row * LANES, (row + 1) * LANES)
-        out_ref[:, part] = (known_ref[pl.ds(row, PAIRS, stride=rows), :] - norm_ref[:1, part]) * BACK
-
-
-def finish(known, norms):
+def join_kernel(mine_ref, others_ref, out_ref):
+    mine = mine_ref[...]
+    other = jnp.where(lax.axis_index("core") == 0, others_ref[1], others_ref[0])
+    best = jnp.maximum(mine, other)
+    out_ref[...] = best + jnp.log2(jnp.exp2(mine - best) + jnp.exp2(other - best))
+
+
+def join(mine, others):
+    return pl.pallas_call(
+        join_kernel,
+        out_shape=jax.ShapeDtypeStruct(mine.shape, jnp.float32),
+        compiler_params=pltpu.CompilerParams(vmem_limit_bytes=4 * 1024 * 1024),
+    )(mine, others)
+
+
+def finish_kernel(*refs):
+    inputs, outs, values, sems = refs[:4], refs[4:6], refs[6:8], refs[8]
+    saves = []
+    for side in range(2):
+        known_ref, norm_ref = inputs[2 * side : 2 * side + 2]
+        count = norm_ref.shape[1]
+        for group in range(PAIRS // GROUP):
+            pairs = slice(group * GROUP, (group + 1) * GROUP)
+            for column in range(count // LANES):
+                part = slice(column * LANES, (column + 1) * LANES)
+                known = known_ref[tile_rows(group, column, count), :]
+                values[side][pairs, part] = (known - norm_ref[:, part]) * BACK
+            save = pltpu.make_async_copy(values[side].at[pairs], outs[side].at[pairs], sems.at[len(saves)])
+            save.start()
+            saves.append(save)
+    for save in saves:
+        save.wait()
+
+
+def finish(source_known, source_norms, target_known, target_norms):
+    shapes = [(PAIRS, norms.shape[1]) for norms in (source_norms, target_norms)]
     return pl.pallas_call(
         finish_kernel,
-        out_shape=jax.ShapeDtypeStruct((PAIRS, norms.shape[1]), jnp.float32),
+        out_shape=[jax.ShapeDtypeStruct(shape, jnp.float32) for shape in shapes],
+        out_specs=[HBM] * 2,
+        scratch_shapes=[pltpu.VMEM(shape, jnp.float32) for shape in shapes]
+        + [pltpu.SemaphoreType.DMA((2 * PAIRS // GROUP,))],
         compiler_params=pltpu.CompilerParams(vmem_limit_bytes=4 * 1024 * 1024),
-    )(known, norms)
+    )(source_known, source_norms, target_known, target_norms)
 
 
 def exchange(value, axes):
@@ -321,11 +369,13 @@
     return exchange(combine(mine, near), NEAR).reshape(rows, LANES)
 
 
-def over_sources(parts, sizes):
-    group = sizes["yh"] * sizes["x"] * sizes["core"]
-    rows = parts.shape[0]
-    mine = exchange(parts.reshape(group, rows // group, LANES), SRC)
-    return exchange(combine(mine, group), SRC).reshape(rows, LANES)
+def over_sources(mine, other, sizes):
+    group = sizes["yh"] * sizes["x"]
+    rows = mine.shape[0]
+    mine = join(mine, lax.all_gather(other, "core"))
+    mine = exchange(mine.reshape(group, rows // group, LANES), CHIPS)
+    half = exchange(combine(mine, group), CHIPS).reshape(rows, LANES)
+    return lax.all_gather(half, "core").reshape(2 * rows, LANES)
 
 
 def body(sizes, source, target, log_source, log_target):
@@ -335,12 +385,10 @@
     )
     for step in range(ITERS):
         if step:
-            (parts,) = next_update(source, target, log_target, known, kept, True)
-        known = over_targets(parts, sizes)
-        norms = source_norms if step == ITERS - 1 else None
-        parts, *rest = next_update(target, source, log_source, known, kept, False, norms)
-        known = over_sources(parts, sizes)
-    return (rest[0], finish(known, target_norms))
+            (parts,) = next_update(source, target, log_target, target_known, kept, True)
+        source_known = over_targets(parts, sizes)
+        target_known = over_sources(*next_update(target, source, log_source, source_known, kept, False), sizes)
+    return finish(source_known, source_norms, target_known, target_norms)
 
 
 def solution(mesh):

time: 182 us -> 211 us (1.16)
  the two profiles are of different devices: /device:TPU:200 before, /device:TPU:65 now
where the time goes in v4:
time: 211 us
  blocking collectives  195 us (92%)
  Pallas kernels  14.4 us (7%)
    all_to_all x10, blocking collectives, exchange(): return lax.all_to_all(value, axes, 0, 0)  174 us
    all_gather x2, blocking collectives, over_sources(): mine = join(mine, lax.all_gather(other, 'core'))  12.6 us
    all_gather x2, blocking collectives, over_sources(): return lax.all_gather(half, 'core').reshape(2 * rows, LANES)  9.02 us
    pallas_call x1, Pallas kernels, first_update(): pl.pallas_call(first_kernel, out_shape=[jax.ShapeDtypeStruct((PAIRS * cel...  6.53 us
    pallas_call x3, Pallas kernels, next_update(): pl.pallas_call(functools.partial(next_kernel, to_source), out_shape=[jax....  6.48 us

profile of v4, /device:TPU:65, one launch (start us, length us, event | category | flops | bytes accessed | tf_op | source)
XLA Modules:
  0.0 210.5 jit_solution(12011922741822388484)
XLA Ops:
  0.6 6.5 %shard_map.59 = (f32[256,128]{1,0:T(8,128)S(1)}, bf16[1024,4096]{1,0:T(8,128)(2,1)S(1)}, f32[8,1024]{1,0:T(8,128)S(1)}, f32[8,4096]{1,0:T(8,128)S(1)}, f32[8,409...) custom-call(bf16[64,4096]{1,0:T(8,128)(2,1)} %bitcast.25, ...), custom_call_target="tpu_custom_call" | custom-call | tf_op jit(solution)/shard_map/pallas_call | solution.py:249
  7.2 9.7 %all_to_all.50.parts_ref = f32[8,32,128]{2,1,0:T(8,128)S(1)} all-to-all(f32[8,32,128]{2,1,0:T(8,128)S(1)} %bitcast.24), channel_id=1, replica_groups=mesh['yh'=2,'x'=4,'core'=2,'zh'=4,'zl'=4,'yl'=2] {'zl','yl'}, dimensions={0} | all-to-all | bytes 262144 | tf_op jit(solution)/shard_map/all_to_all | solution.py:361
  16.9 24.3 %all_to_all.51.parts_ref = f32[4,32,128]{2,1,0:T(8,128)S(1)} all-to-all(f32[4,32,128]{2,1,0:T(8,128)S(1)} %shard_map.60), channel_id=1, replica_groups=mesh['yh'=2,'x'=4,'core'=2,'zh'=4,'zl'=4,'yl'=2] {'zh'}, dimensions={0} | all-to-all | bytes 131072 | tf_op jit(solution)/shard_map/all_to_all | solution.py:361
  41.3 7.9 %all_to_all.52 = f32[8,32,128]{2,1,0:T(8,128)S(1)} all-to-all(f32[8,32,128]{2,1,0:T(8,128)S(1)} %shard_map.61), channel_id=1, replica_groups=mesh['yh'=2,'x'=4,'core'=2,'zh'=4,'zl'=4,'yl'=2] {'zl','yl'}, dimensions={0} | all-to-all | bytes 262144 | tf_op jit(solution)/shard_map/all_to_all | solution.py:361
  49.2 1.8 shard_map.62
  51.0 6.6 %all-gather = f32[1024,128]{1,0:T(8,128)S(1)} all-gather(f32[512,128]{1,0:T(8,128)S(1)} %get-tuple-element.21), channel_id=2, replica_groups=mesh['yh'=2,'x'=4,'core'=2,'zh'=4,'zl'=4,'yl'=2] {'core'}, dimensions={0}, use_global_device_ids=true | all-gather | bytes 786432 | tf_op jit(solution)/shard_map/all_gather | solution.py:375
  57.6 0.1 shard_map.63
  57.8 40.5 %all_to_all.53.parts_ref = f32[8,64,128]{2,1,0:T(8,128)S(1)} all-to-all(f32[8,64,128]{2,1,0:T(8,128)S(1)} %bitcast.20), channel_id=1, replica_groups=mesh['yh'=2,'x'=4,'core'=2,'zh'=4,'zl'=4,'yl'=2] {'yh','x'}, dimensions={0} | all-to-all | bytes 524288 | tf_op jit(solution)/shard_map/all_to_all | solution.py:361
  98.3 0.1 shard_map.64
  98.3 10.2 %all_to_all.54 = f32[8,64,128]{2,1,0:T(8,128)S(1)} all-to-all(f32[8,64,128]{2,1,0:T(8,128)S(1)} %shard_map.64), channel_id=1, replica_groups=mesh['yh'=2,'x'=4,'core'=2,'zh'=4,'zl'=4,'yl'=2] {'yh','x'}, dimensions={0} | all-to-all | bytes 524288 | tf_op jit(solution)/shard_map/all_to_all | solution.py:361
  108.5 4.5 %all_gather.20 = f32[2,512,128]{2,1,0:T(8,128)S(1)} all-gather(f32[1,512,128]{2,1,0:T(8,128)S(1)} %bitcast.33), channel_id=1, replica_groups=mesh['yh'=2,'x'=4,'core'=2,'zh'=4,'zl'=4,'yl'=2] {'core'}, dimensions={0}, use_global_device_ids=true | all-gather | bytes 786432 | tf_op jit(solution)/shard_map/all_gather | solution.py:378
  113.0 2.9 %shard_map.65 = f32[256,128]{1,0:T(8,128)S(1)} custom-call(bf16[64,1024]{1,0:T(8,128)(2,1)} %bitcast.31, bf16[64,4096]{1,0:T(8,128)(2,1)} %bitcast.27, f32[32,4096]{1,0:T(8,128)S(1)} %get-tuple-element.14.refs_2_, f32[1024,128]{1,0:T(8,128)S(1)} %bitcast.14, bf16[1024,4096]{1,0:T(8,128)(2,1)S(1)} %get-tuple-element.17.refs_4_, ...), custom_call_target="tpu_custom_call" | custom-call | tf_op jit(solution)/shard_map/pallas_call | solution.py:279
  115.9 7.6 %all_to_all.55.parts_ref = f32[8,32,128]{2,1,0:T(8,128)S(1)} all-to-all(f32[8,32,128]{2,1,0:T(8,128)S(1)} %bitcast.23), channel_id=1, replica_groups=mesh['yh'=2,'x'=4,'core'=2,'zh'=4,'zl'=4,'yl'=2] {'zl','yl'}, dimensions={0} | all-to-all | bytes 262144 | tf_op jit(solution)/shard_map/all_to_all | solution.py:361
  123.6 15.6 %all_to_all.56.parts_ref = f32[4,32,128]{2,1,0:T(8,128)S(1)} all-to-all(f32[4,32,128]{2,1,0:T(8,128)S(1)} %shard_map.66), channel_id=1, replica_groups=mesh['yh'=2,'x'=4,'core'=2,'zh'=4,'zl'=4,'yl'=2] {'zh'}, dimensions={0} | all-to-all | bytes 131072 | tf_op jit(solution)/shard_map/all_to_all | solution.py:361
  139.2 9.1 %all_to_all.57 = f32[8,32,128]{2,1,0:T(8,128)S(1)} all-to-all(f32[8,32,128]{2,1,0:T(8,128)S(1)} %shard_map.67), channel_id=1, replica_groups=mesh['yh'=2,'x'=4,'core'=2,'zh'=4,'zl'=4,'yl'=2] {'zl','yl'}, dimensions={0} | all-to-all | bytes 262144 | tf_op jit(solution)/shard_map/all_to_all | solution.py:361
  148.3 1.8 shard_map.68
  150.1 6.0 %all-gather.1 = f32[1024,128]{1,0:T(8,128)S(1)} all-gather(f32[512,128]{1,0:T(8,128)S(1)} %get-tuple-element.24), channel_id=3, replica_groups=mesh['yh'=2,'x'=4,'core'=2,'zh'=4,'zl'=4,'yl'=2] {'core'}, dimensions={0}, use_global_device_ids=true | all-gather | bytes 786432 | tf_op jit(solution)/shard_map/all_gather | solution.py:375
  156.1 0.1 shard_map.69
  156.2 38.5 %all_to_all.58.parts_ref = f32[8,64,128]{2,1,0:T(8,128)S(1)} all-to-all(f32[8,64,128]{2,1,0:T(8,128)S(1)} %bitcast.21), channel_id=1, replica_groups=mesh['yh'=2,'x'=4,'core'=2,'zh'=4,'zl'=4,'yl'=2] {'yh','x'}, dimensions={0} | all-to-all | bytes 524288 | tf_op jit(solution)/shard_map/all_to_all | solution.py:361
  194.7 0.1 shard_map.70
  194.8 10.2 %all_to_all.59 = f32[8,64,128]{2,1,0:T(8,128)S(1)} all-to-all(f32[8,64,128]{2,1,0:T(8,128)S(1)} %shard_map.70), channel_id=1, replica_groups=mesh['yh'=2,'x'=4,'core'=2,'zh'=4,'zl'=4,'yl'=2] {'yh','x'}, dimensions={0} | all-to-all | bytes 524288 | tf_op jit(solution)/shard_map/all_to_all | solution.py:361
  205.0 4.5 %all_gather.23 = f32[2,512,128]{2,1,0:T(8,128)S(1)} all-gather(f32[1,512,128]{2,1,0:T(8,128)S(1)} %bitcast.34), channel_id=1, replica_groups=mesh['yh'=2,'x'=4,'core'=2,'zh'=4,'zl'=4,'yl'=2] {'core'}, dimensions={0}, use_global_device_ids=true | all-gather | bytes 786432 | tf_op jit(solution)/shard_map/all_gather | solution.py:378
  209.5 0.9 shard_map.71
  (4 shorter events, 0.1 us)

commit v5 on v4

--- a/solution.py
+++ b/solution.py
@@ -24,10 +24,9 @@
 BACK = -entropy / LOG2E
 SMALL = 2.0**-90
 
-NEAR = ("zl", "yl")
-FAR = ("zh",)
-CHIPS = ("yh", "x")
-SRC = CHIPS + ("core",)
+NEAR = ("z0", "yl", "z1")
+FAR = ("z2", "z3")
+CHIPS = ("x", "yh")
 
 TILE = 256
 CHUNK = 512
@@ -357,20 +356,24 @@
     )(source_known, source_norms, target_known, target_norms)
 
 
+def count(sizes, axes):
+    return math.prod(sizes[axis] for axis in axes)
+
+
 def exchange(value, axes):
     return lax.all_to_all(value, axes, 0, 0)
 
 
 def over_targets(parts, sizes):
-    near = sizes["zl"] * sizes["yl"]
+    near, far = count(sizes, NEAR), count(sizes, FAR)
     rows = parts.shape[0]
     mine = exchange(parts.reshape(near, rows // near, LANES), NEAR)
-    mine = exchange(combine(mine, sizes["zh"]), FAR)
+    mine = exchange(combine(mine, far), FAR)
     return exchange(combine(mine, near), NEAR).reshape(rows, LANES)
 
 
 def over_sources(mine, other, sizes):
-    group = sizes["yh"] * sizes["x"]
+    group = count(sizes, CHIPS)
     rows = mine.shape[0]
     mine = join(mine, lax.all_gather(other, "core"))
     mine = exchange(mine.reshape(group, rows // group, LANES), CHIPS)
@@ -392,9 +395,9 @@
 
 
 def solution(mesh):
-    sizes = {"yh": 2, "x": 4, "core": 2, "zh": 4, "zl": 4, "yl": 2}
+    sizes = {"yh": 2, "x": 4, "core": 2, "z3": 2, "z2": 2, "z1": 2, "z0": 2, "yl": 2}
     fine = Mesh(mesh.devices.reshape(tuple(sizes.values())), tuple(sizes))
-    src, tgt = SRC, FAR + NEAR
+    src, tgt = ("yh", "x", "core"), ("z3", "z2", "z1", "z0", "yl")
     in_specs = (P(src, None), P(tgt, None), P(None, src), P(None, tgt))
     out_specs = (P(None, src), P(None, tgt))
     return jax.shard_map(

time: 211 us -> 207 us (0.981)
  the two profiles are of different devices: /device:TPU:65 before, /device:TPU:73 now
where the time goes in v5:
time: 207 us; the launch traced here: 210 us
  blocking collectives  194 us (94%)
  Pallas kernels  14.4 us (7%)
    all_to_all x10, blocking collectives, exchange(): return lax.all_to_all(value, axes, 0, 0)  174 us
    all_gather x2, blocking collectives, over_sources(): mine = join(mine, lax.all_gather(other, 'core'))  11.9 us
    all_gather x2, blocking collectives, over_sources(): return lax.all_gather(half, 'core').reshape(2 * rows, LANES)  8.8 us
    pallas_call x1, Pallas kernels, first_update(): pl.pallas_call(first_kernel, out_shape=[jax.ShapeDtypeStruct((PAIRS * cel...  6.53 us
    pallas_call x3, Pallas kernels, next_update(): pl.pallas_call(functools.partial(next_kernel, to_source), out_shape=[jax....  6.49 us

profile of v5, /device:TPU:73, one launch (start us, length us, event | category | flops | bytes accessed | tf_op | source)
XLA Modules:
  0.0 209.5 jit_solution(5416307989394654929)
XLA Ops:
  0.6 6.5 %shard_map.59 = (f32[256,128]{1,0:T(8,128)S(1)}, bf16[1024,4096]{1,0:T(8,128)(2,1)S(1)}, f32[8,1024]{1,0:T(8,128)S(1)}, f32[8,4096]{1,0:T(8,128)S(1)}, f32[8,409...) custom-call(bf16[64,4096]{1,0:T(8,128)(2,1)} %bitcast.25, ...), custom_call_target="tpu_custom_call" | custom-call | tf_op jit(solution)/shard_map/pallas_call | solution.py:248
  7.2 9.4 %all_to_all.50.parts_ref = f32[8,32,128]{2,1,0:T(8,128)S(1)} all-to-all(f32[8,32,128]{2,1,0:T(8,128)S(1)} %bitcast.24), channel_id=1, replica_groups=mesh['yh'=2,'x'=4,'core'=2,'z3'=2,'z2'=2,'z1'=2,'z0'=2,'yl'=2] {'z0','yl..., dimensions={0} | all-to-all | bytes 262144 | tf_op jit(solution)/shard_map/all_to_all | solution.py:364
  16.6 23.6 %all_to_all.51.parts_ref = f32[4,32,128]{2,1,0:T(8,128)S(1)} all-to-all(f32[4,32,128]{2,1,0:T(8,128)S(1)} %shard_map.60), channel_id=1, replica_groups=mesh['yh'=2,'x'=4,'core'=2,'z3'=2,'z2'=2,'z1'=2,'z0'=2,'yl'=2] {'z2','z3'}, dimensions={0} | all-to-all | bytes 131072 | tf_op jit(solution)/shard_map/all_to_all | solution.py:364
  40.2 8.6 %all_to_all.52 = f32[8,32,128]{2,1,0:T(8,128)S(1)} all-to-all(f32[8,32,128]{2,1,0:T(8,128)S(1)} %shard_map.61), channel_id=1, replica_groups=mesh['yh'=2,'x'=4,'core'=2,'z3'=2,'z2'=2,'z1'=2,'z0'=2,'yl'=2] {'z0','yl..., dimensions={0} | all-to-all | bytes 262144 | tf_op jit(solution)/shard_map/all_to_all | solution.py:364
  48.9 1.8 shard_map.62
  50.7 6.3 %all-gather = f32[1024,128]{1,0:T(8,128)S(1)} all-gather(f32[512,128]{1,0:T(8,128)S(1)} %get-tuple-element.21), channel_id=2, replica_groups=mesh['yh'=2,'x'=4,'core'=2,'z3'=2,'z2'=2,'z1'=2,'z0'=2,'yl'=2] {'core'}, dimensions={0}, use_global_device_ids=true | all-gather | bytes 786432 | tf_op jit(solution)/shard_map/all_gather | solution.py:378
  56.9 0.1 shard_map.63
  57.1 13.0 %all_to_all.53.parts_ref = f32[8,64,128]{2,1,0:T(8,128)S(1)} all-to-all(f32[8,64,128]{2,1,0:T(8,128)S(1)} %bitcast.20), channel_id=1, replica_groups=mesh['yh'=2,'x'=4,'core'=2,'z3'=2,'z2'=2,'z1'=2,'z0'=2,'yl'=2] {'x','yh'}, dimensions={0} | all-to-all | bytes 524288 | tf_op jit(solution)/shard_map/all_to_all | solution.py:364
  70.1 0.1 shard_map.64
  70.1 10.7 %all_to_all.54 = f32[8,64,128]{2,1,0:T(8,128)S(1)} all-to-all(f32[8,64,128]{2,1,0:T(8,128)S(1)} %shard_map.64), channel_id=1, replica_groups=mesh['yh'=2,'x'=4,'core'=2,'z3'=2,'z2'=2,'z1'=2,'z0'=2,'yl'=2] {'x','yh'}, dimensions={0} | all-to-all | bytes 524288 | tf_op jit(solution)/shard_map/all_to_all | solution.py:364
  80.8 4.4 %all_gather.20 = f32[2,512,128]{2,1,0:T(8,128)S(1)} all-gather(f32[1,512,128]{2,1,0:T(8,128)S(1)} %bitcast.33), channel_id=1, replica_groups=mesh['yh'=2,'x'=4,'core'=2,'z3'=2,'z2'=2,'z1'=2,'z0'=2,'yl'=2] {'core'}, dimensions={0}, use_global_device_ids=true | all-gather | bytes 786432 | tf_op jit(solution)/shard_map/all_gather | solution.py:381
  85.2 2.9 %shard_map.65 = f32[256,128]{1,0:T(8,128)S(1)} custom-call(bf16[64,1024]{1,0:T(8,128)(2,1)} %bitcast.31, bf16[64,4096]{1,0:T(8,128)(2,1)} %bitcast.27, f32[32,4096]{1,0:T(8,128)S(1)} %get-tuple-element.14.refs_2_, f32[1024,128]{1,0:T(8,128)S(1)} %bitcast.14, bf16[1024,4096]{1,0:T(8,128)(2,1)S(1)} %get-tuple-element.17.refs_4_, ...), custom_call_target="tpu_custom_call" | custom-call | tf_op jit(solution)/shard_map/pallas_call | solution.py:278
  88.1 9.8 %all_to_all.55.parts_ref = f32[8,32,128]{2,1,0:T(8,128)S(1)} all-to-all(f32[8,32,128]{2,1,0:T(8,128)S(1)} %bitcast.23), channel_id=1, replica_groups=mesh['yh'=2,'x'=4,'core'=2,'z3'=2,'z2'=2,'z1'=2,'z0'=2,'yl'=2] {'z0','yl..., dimensions={0} | all-to-all | bytes 262144 | tf_op jit(solution)/shard_map/all_to_all | solution.py:364
  97.9 40.7 %all_to_all.56.parts_ref = f32[4,32,128]{2,1,0:T(8,128)S(1)} all-to-all(f32[4,32,128]{2,1,0:T(8,128)S(1)} %shard_map.66), channel_id=1, replica_groups=mesh['yh'=2,'x'=4,'core'=2,'z3'=2,'z2'=2,'z1'=2,'z0'=2,'yl'=2] {'z2','z3'}, dimensions={0} | all-to-all | bytes 131072 | tf_op jit(solution)/shard_map/all_to_all | solution.py:364
  138.6 8.8 %all_to_all.57 = f32[8,32,128]{2,1,0:T(8,128)S(1)} all-to-all(f32[8,32,128]{2,1,0:T(8,128)S(1)} %shard_map.67), channel_id=1, replica_groups=mesh['yh'=2,'x'=4,'core'=2,'z3'=2,'z2'=2,'z1'=2,'z0'=2,'yl'=2] {'z0','yl..., dimensions={0} | all-to-all | bytes 262144 | tf_op jit(solution)/shard_map/all_to_all | solution.py:364
  147.5 1.8 shard_map.68
  149.3 5.6 %all-gather.1 = f32[1024,128]{1,0:T(8,128)S(1)} all-gather(f32[512,128]{1,0:T(8,128)S(1)} %get-tuple-element.24), channel_id=3, replica_groups=mesh['yh'=2,'x'=4,'core'=2,'z3'=2,'z2'=2,'z1'=2,'z0'=2,'yl'=2] {'core'}, dimensions={0}, use_global_device_ids=true | all-gather | bytes 786432 | tf_op jit(solution)/shard_map/all_gather | solution.py:378
  154.9 0.1 shard_map.69
  155.0 38.3 %all_to_all.58.parts_ref = f32[8,64,128]{2,1,0:T(8,128)S(1)} all-to-all(f32[8,64,128]{2,1,0:T(8,128)S(1)} %bitcast.21), channel_id=1, replica_groups=mesh['yh'=2,'x'=4,'core'=2,'z3'=2,'z2'=2,'z1'=2,'z0'=2,'yl'=2] {'x','yh'}, dimensions={0} | all-to-all | bytes 524288 | tf_op jit(solution)/shard_map/all_to_all | solution.py:364
  193.3 0.1 shard_map.70
  193.4 10.7 %all_to_all.59 = f32[8,64,128]{2,1,0:T(8,128)S(1)} all-to-all(f32[8,64,128]{2,1,0:T(8,128)S(1)} %shard_map.70), channel_id=1, replica_groups=mesh['yh'=2,'x'=4,'core'=2,'z3'=2,'z2'=2,'z1'=2,'z0'=2,'yl'=2] {'x','yh'}, dimensions={0} | all-to-all | bytes 524288 | tf_op jit(solution)/shard_map/all_to_all | solution.py:364
  204.1 4.4 %all_gather.23 = f32[2,512,128]{2,1,0:T(8,128)S(1)} all-gather(f32[1,512,128]{2,1,0:T(8,128)S(1)} %bitcast.34), channel_id=1, replica_groups=mesh['yh'=2,'x'=4,'core'=2,'z3'=2,'z2'=2,'z1'=2,'z0'=2,'yl'=2] {'core'}, dimensions={0}, use_global_device_ids=true | all-gather | bytes 786432 | tf_op jit(solution)/shard_map/all_gather | solution.py:381
  208.5 0.9 shard_map.71
  (4 shorter events, 0.1 us)
